TPU v7x, 32 devices: a whole 2x2x4 slice. The times are simulated.
32 devices in a mesh: grp: 2 (over core), blk: 16 (over z, y, x).
Axes of the slice: x: 2, y: 2, z: 4, core: 2. Of those that a mesh axis runs over, the one named last changes fastest.
Arguments:
- queries: bfloat16 [8192, 2048], P(('grp', 'blk')), may hold values from -6 to 6
- keys: bfloat16 [8192, 2048], P(('grp', 'blk')), may hold values from -6 to 6
- values: bfloat16 [8192, 2048], P(('grp', 'blk')), may hold values from -6 to 6
- memory_keys: bfloat16 [256, 64, 2048], P(('grp', 'blk')), may hold values from -6 to 6
- memory_values: bfloat16 [256, 64, 2048], P(('grp', 'blk')), may hold values from -6 to 6
- owners: int32 [64, 16, 8], P(('grp', 'blk')), may hold values from 0 to 31, all different within a row; in each aligned block of 32 rows (0 to 31, 32 to 63, ..., all dimensions but the last counted through in order) at most 10 rows name the same one
- slots: int32 [64, 16, 8], P(('grp', 'blk')), may hold values from 0 to 7
- gate_logit: float32 [16], replicated, may hold values from -2 to 2
Outputs:
- mixed: bfloat16 [8192, 2048], P(('grp', 'blk'))
Inputs may be any that keep to these rules, and one draw needn't show every extreme that they name: Each pair of a query block and a head names 8 different owners; the rows of one device name any one owner 10 times at most, and on some devices some owner exactly 10 times.
All inputs are finite; a program needn't handle non-finite values.
Results may differ from a plain program's by a relative error of at most 0.005.
Values may be sent and summed in bfloat16 or wider, within the bound.
A program may use at most 128 MiB of HBM per device.

v0:
```python
import math

import jax
import jax.numpy as jnp
from jax import lax
from jax.sharding import PartitionSpec as P

H = 16
QBLK = 128


masked_score = -1e30


def from_behind(value, axis, steps):
    count = lax.axis_size(axis)
    initial, last = (max(0, -steps), min(count, count - steps))
    return lax.ppermute(value, axis, [(source, source + steps) for source in range(initial, last)])


def pick_blocks(key_mem, value_mem, requests, head_count):
    clamped = jnp.maximum(requests, 0)
    block_of = clamped // head_count
    head_of = clamped % head_count
    blocks, block_rows, model_width = key_mem.shape
    head_size = model_width // head_count
    key_heads = key_mem.reshape(blocks, block_rows, head_count, head_size)
    value_heads = value_mem.reshape(blocks, block_rows, head_count, head_size)
    picked_keys = key_heads[block_of, :, head_of, :]
    picked_values = value_heads[block_of, :, head_of, :]
    return jnp.concatenate([picked_keys, picked_values], axis=-1)


def plan_requests(target, local_code, peer_count, peer_slots):
    request_count = target.shape[0]
    order = jnp.arange(request_count, dtype=jnp.int32)
    same_target = (target[:, None] == target[None, :]) & (order[None, :] < order[:, None])
    slot_rank = jnp.sum(same_target.astype(jnp.int32), axis=1)
    arrival = target * peer_slots + slot_rank
    requests = jnp.full((peer_count * peer_slots,), -1, jnp.int32).at[arrival].set(local_code)
    return (requests.reshape(peer_count, peer_slots), arrival)


def local(queries, keys, values, memory_keys, memory_values, owners, slots, gate_logit):
    row_count, model_width = queries.shape
    head_size = model_width // H
    score_scale = 1.0 / math.sqrt(head_size)
    own_pair = jnp.concatenate([keys, values], axis=1)
    earlier = []
    moving = own_pair
    for distance in range(3):
        moving = from_behind(moving, "blk", 1)
        earlier.insert(0, moving)
    context = jnp.concatenate(earlier + [own_pair], axis=0)
    position = lax.axis_index("blk")
    query_pos = jnp.arange(row_count, dtype=jnp.int32)
    context_pos = jnp.arange(4 * row_count, dtype=jnp.int32)
    key_pos = (position - 3) * row_count + context_pos
    offset = 3 * row_count + query_pos[:, None] - context_pos[None, :]
    allowed = (key_pos[None, :] >= 0) & (offset >= 0) & (offset <= 3 * row_count)

    def attend_head(head_index):
        start_col = head_index * head_size
        query_head = lax.dynamic_slice_in_dim(queries, start_col, head_size, 1)
        key_head = lax.dynamic_slice_in_dim(context, start_col, head_size, 1)
        value_head = lax.dynamic_slice_in_dim(context, model_width + start_col, head_size, 1)
        scores = (
            lax.dot_general(
                query_head, key_head, (((1,), (1,)), ((), ())), preferred_element_type=jnp.float32
            )
            * score_scale
        )
        scores = jnp.where(allowed, scores, masked_score)
        row_max = jnp.max(scores, axis=1, keepdims=True)
        raised = jnp.exp(scores - row_max)
        weights = (raised / jnp.sum(raised, axis=1, keepdims=True)).astype(jnp.bfloat16)
        return jnp.dot(weights, value_head, preferred_element_type=jnp.float32)

    band_out = lax.map(attend_head, jnp.arange(H, dtype=jnp.int32))
    band_out = jnp.transpose(band_out, (1, 0, 2))
    query_blocks = row_count // QBLK
    target_owner = owners.reshape(-1)
    slot_flat = slots.reshape(-1)
    head_flat = jnp.broadcast_to(
        jnp.arange(H, dtype=jnp.int32)[None, :, None], owners.shape
    ).reshape(-1)
    grp_count = lax.axis_size("grp")
    blk_count = lax.axis_size("blk")
    capacity = max(2, 5 * target_owner.shape[0] // (4 * grp_count * blk_count))
    peer_count = grp_count * blk_count
    requests, arrival = plan_requests(target_owner, slot_flat * H + head_flat, peer_count, capacity)
    arrived = lax.all_to_all(
        pick_blocks(
            memory_keys,
            memory_values,
            lax.all_to_all(requests, ("grp", "blk"), split_axis=0, concat_axis=0, tiled=True),
            H,
        ),
        ("grp", "blk"),
        split_axis=0,
        concat_axis=0,
        tiled=True,
    )
    arrived_flat = arrived.reshape(peer_count * capacity, arrived.shape[-2], arrived.shape[-1])
    picked = arrived_flat[arrival].reshape(owners.shape + arrived.shape[-2:])
    query_tiles = queries.reshape(query_blocks, QBLK, H, head_size)
    scores = (
        jnp.einsum(
            "bqhd,bhrkd->bhqrk",
            query_tiles,
            picked[..., :head_size],
            preferred_element_type=jnp.float32,
        )
        * score_scale
    )
    row_max = jnp.max(scores, axis=(3, 4), keepdims=True)
    raised = jnp.exp(scores - row_max)
    weights = (raised / jnp.sum(raised, axis=(3, 4), keepdims=True)).astype(jnp.bfloat16)
    memory_out = jnp.einsum(
        "bhqrk,bhrkd->bqhd", weights, picked[..., head_size:], preferred_element_type=jnp.float32
    )
    memory_out = memory_out.reshape(row_count, H, head_size)
    gate_share = jax.nn.sigmoid(gate_logit)[None, :, None]
    mixed = gate_share * memory_out + (1.0 - gate_share) * band_out
    return mixed.reshape(row_count, model_width).astype(jnp.bfloat16)


def solution(mesh):
    return jax.shard_map(
        local,
        mesh=mesh,
        in_specs=(
            P(("grp", "blk"), None),
            P(("grp", "blk"), None),
            P(("grp", "blk"), None),
            P(("grp", "blk"), None, None),
            P(("grp", "blk"), None, None),
            P(("grp", "blk"), None, None),
            P(("grp", "blk"), None, None),
            P(),
        ),
        out_specs=P(("grp", "blk"), None),
        check_vma=False,
    )
```

profile of v0, /device:TPU:17, one launch (start us, length us, event | category | flops | bytes accessed | tf_op | source)
XLA Modules:
  0.0 606.4 jit_solution(5692128249953450305)
XLA Ops:
  5.1 6.2 %all-to-all-start = ((s32[32,1,10]{2,1,0:T(1,128)}), s32[32,1,10]{2,1,0:T(1,128)S(1)}, u32[]{:S(2)}, u32[]{:S(2)}) async-start(s32[32,1,10]{2,1,0:T(1,128)} %bitcast.2), calls=%async_computation | async-start | bytes 32768 | tf_op jit(solution)/shard_map/all_to_all | solution.py:96
  16.2 6.7 %gather_fusion = bf16[320,64,128]{2,1,0:T(8,128)(2,1)} fusion(bf16[8,64,16,128]{3,1,2,0:T(8,128)(2,1)} %copy_bitcast_fusion.1, s32[320]{0:T(512)S(1)} %reshape.165), kind=kCustom, calls=%fused_computation | custom fusion | bytes 10488320 | tf_op jit(solution)/shard_map/gather | solution.py:29
  22.9 6.6 %gather_fusion.1 = bf16[320,64,128]{2,1,0:T(8,128)(2,1)} fusion(bf16[8,64,16,128]{3,1,2,0:T(8,128)(2,1)} %copy_bitcast_fusion, s32[320]{0:T(512)S(1)} %reshape.165), kind=kCustom, calls=%fused_computation.1 | custom fusion | bytes 10488320 | tf_op jit(solution)/shard_map/gather | solution.py:30
  29.5 10.7 %pad_maximum_fusion = bf16[32,10,64,256]{3,2,1,0:T(8,128)(2,1)} fusion(bf16[32,10,64,128]{3,2,1,0:T(8,128)(2,1)} %bitcast.86, bf16[32,10,64,128]{3,2,1,0:T(8,128)(2,1)} %bitcast.85), kind=kLoop, calls=%fused_computation.21 | loop fusion | flops 20971520 | bytes 20971520 | tf_op jit(solution)/shard_map/concatenate | solution.py:31
  40.2 6.2 %all-to-all-start.1 = ((bf16[32,10,64,256]{3,2,1,0:T(8,128)(2,1)}), bf16[32,10,64,256]{3,2,1,0:T(8,128)(2,1)}, u32[]{:S(2)}, u32[]{:S(2)}) async-start(bf16[32,10,64,256]{3,2,1,0:T(8,128)(2,1)} %pad_maximum_fusion), calls=%async_computation.1 | async-start | bytes 20971520 | tf_op jit(solution)/shard_map/all_to_all | solution.py:92
  51.0 274.6 %collective-permute-done = bf16[256,4096]{1,0:T(8,128)(2,1)S(1)} collective-permute-done((bf16[256,4096]{1,0:T(8,128)(2,1)S(1)}, bf16[256,4096]{1,0:T(8,128)(2,1)S(1)}, u32[]{:S(2)}, u32[]{:S(2)}) %collective-permute-start) | collective-permute-done | bytes 2097184 | tf_op jit(solution)/shard_map/ppermute | solution.py:18
  328.8 48.6 %collective-permute-done.1 = bf16[256,4096]{1,0:T(8,128)(2,1)} collective-permute-done((bf16[256,4096]{1,0:T(8,128)(2,1)S(1)}, bf16[256,4096]{1,0:T(8,128)(2,1)}, u32[]{:S(2)}, u32[]{:S(2)}) %collective-permute-start.1) | collective-permute-done | bytes 2097184 | tf_op jit(solution)/shard_map/ppermute | solution.py:18
  382.3 45.0 %collective-permute-done.2 = bf16[256,4096]{1,0:T(8,128)(2,1)} collective-permute-done((bf16[256,4096]{1,0:T(8,128)(2,1)}, bf16[256,4096]{1,0:T(8,128)(2,1)}, u32[]{:S(2)}, u32[]{:S(2)}) %collective-permute-start.2) | collective-permute-done | bytes 2097184 | tf_op jit(solution)/shard_map/ppermute | solution.py:18
  427.3 6.5 %pad_maximum_fusion.1 = bf16[1024,4096]{1,0:T(8,128)(2,1)} fusion(bf16[256,4096]{1,0:T(8,128)(2,1)S(1)} %constant_dynamic-update-slice_fusion, bf16[256,4096]{1,0:T(8,128)(2,1)} %copy-done.5, bf16[256,4096]{1,0:T(8,128)(2,1)} %collective-permute-done.1, bf16[256,4096]{1,0:T(8,128)(2,1)} %collective-permute-done.2), kind=kLoop, calls=%fused_computation.22 | loop fusion | flops 33554432 | bytes 16777216 | tf_op jit(solution)/shard_map/concatenate | solution.py:54
  433.8 148.7 %while.13 = (s32[]{:T(128)}, f32[16,256,128]{2,0,1:T(8,128)}, s32[16]{0:T(128)S(1)}, bf16[256,2048]{1,0:T(8,128)(2,1)}, bf16[1024,4096]{1,0:T(8,128)(2,1)}, /*in...) while((s32[]{:T(128)}, f32[16,256,128]{2,0,1:T(8,128)}, ...), condition=%wide.region_7.8_spmd.clone, body=%wide.region_4.7_spmd.clone.sunk | while | flops 137625088 | bytes 4136194 | solution.py:79
  438.5 4.7 dynamic_update_slice.9
  447.8 4.7 dynamic_update_slice.9
  457.1 4.7 dynamic_update_slice.9
  466.4 4.7 dynamic_update_slice.9
  475.7 4.7 dynamic_update_slice.9
  485.0 4.7 dynamic_update_slice.9
  494.3 4.7 dynamic_update_slice.9
  503.6 4.7 dynamic_update_slice.9
  512.9 4.7 dynamic_update_slice.9
  522.2 4.7 dynamic_update_slice.9
  531.5 4.7 dynamic_update_slice.9
  550.1 4.7 dynamic_update_slice.9
  568.6 4.7 dynamic_update_slice.9
  582.6 12.7 %gather_fusion.2 = bf16[256,64,256]{2,1,0:T(8,128)(2,1)} fusion(bf16[320,64,256]{2,1,0:T(8,128)(2,1)} %bitcast.12, s32[1024]{0:T(1024)S(1)} %pad_clamp_fusion), kind=kCustom, calls=%fused_computation.2 | custom fusion | bytes 16778240 | tf_op jit(solution)/shard_map/gather | solution.py:105
  (127 shorter events, 109.6 us)
Async XLA Ops:
  0.0 11.3 %copy-start = (bf16[8,64,2048]{2,1,0:T(8,128)(2,1)S(1)}, bf16[8,64,2048]{2,1,0:T(8,128)(2,1)}, u32[]{:S(2)}) copy-start(bf16[8,64,2048]{2,1,0:T(8,128)(2,1)} %param.13) | copy-start | bytes 6291460
  5.1 10.9 %all-to-all-start = ((s32[32,1,10]{2,1,0:T(1,128)}), s32[32,1,10]{2,1,0:T(1,128)S(1)}, u32[]{:S(2)}, u32[]{:S(2)}) async-start(s32[32,1,10]{2,1,0:T(1,128)} %bitcast.2), calls=%async_computation | async-start | bytes 32768 | tf_op jit(solution)/shard_map/all_to_all | solution.py:96
  11.3 1.9 copy-start.3
  40.2 6.2 %copy-start.6 = (bf16[256,2048]{1,0:T(8,128)(2,1)S(1)}, bf16[256,2048]{1,0:T(8,128)(2,1)}, u32[]{:S(2)}) copy-start(bf16[256,2048]{1,0:T(8,128)(2,1)} %param.11) | copy-start | bytes 3145732
  40.2 542.4 %all-to-all-start.1 = ((bf16[32,10,64,256]{3,2,1,0:T(8,128)(2,1)}), bf16[32,10,64,256]{3,2,1,0:T(8,128)(2,1)}, u32[]{:S(2)}, u32[]{:S(2)}) async-start(bf16[32,10,64,256]{3,2,1,0:T(8,128)(2,1)} %pad_maximum_fusion), calls=%async_computation.1 | async-start | bytes 20971520 | tf_op jit(solution)/shard_map/all_to_all | solution.py:92
  46.4 334.6 %copy-start.7 = (f32[16]{0:T(128)S(1)}, f32[16]{0:T(128)}, u32[]{:S(2)}) copy-start(f32[16]{0:T(128)} %param.17) | copy-start | bytes 196
  47.9 277.7 %collective-permute-start = (bf16[256,4096]{1,0:T(8,128)(2,1)S(1)}, bf16[256,4096]{1,0:T(8,128)(2,1)S(1)}, u32[]{:S(2)}, u32[]{:S(2)}) collective-permute-start(bf16[256,4096]{1,0:T(8,128)(2,1)S(1)} %constant_dynamic-update-slice_fusion), channel_id=1, source_target_pairs={{0,1},{1,2},{2,3},{3,4},{4,5},{5,6},{6,7},{7,8},{8,9},{9,10},{10,1... | collective-permute-start | bytes 6291464 | tf_op jit(solution)/shard_map/ppermute | solution.py:18
  325.6 1.3 copy-start.5
  326.9 50.5 %collective-permute-start.1 = (bf16[256,4096]{1,0:T(8,128)(2,1)S(1)}, bf16[256,4096]{1,0:T(8,128)(2,1)}, u32[]{:S(2)}, u32[]{:S(2)}) collective-permute-start(bf16[256,4096]{1,0:T(8,128)(2,1)S(1)} %collective-permute-done), channel_id=1, source_target_pairs={{0,1},{1,2},{2,3},{3,4},{4,5},{5,6},{6,7},{7,8},{8,9},{9,10},{10,1... | collective-permute-start | bytes 6291464 | tf_op jit(solution)/shard_map/ppermute | solution.py:18
  377.5 49.8 %collective-permute-start.2 = (bf16[256,4096]{1,0:T(8,128)(2,1)}, bf16[256,4096]{1,0:T(8,128)(2,1)}, u32[]{:S(2)}, u32[]{:S(2)}) collective-permute-start(bf16[256,4096]{1,0:T(8,128)(2,1)} %collective-permute-done.1), channel_id=1, source_target_pairs={{0,1},{1,2},{2,3},{3,4},{4,5},{5,6},{6,7},{7,8},{8,9},{9,10},{10,1... | collective-permute-start | bytes 6291464 | tf_op jit(solution)/shard_map/ppermute | solution.py:18
  582.6 12.7 %copy-start.2 = (bf16[2,128,16,128,1]{3,2,1,0,4:T(8,128)(2,1)S(1)}, bf16[2,128,16,128,1]{3,2,1,0,4:T(8,128)(2,1)}, u32[]{:S(2)}) copy-start(bf16[2,128,16,128,1]{3,2,1,0,4:T(8,128)(2,1)} %bitcast_bitcast_fusion) | copy-start | bytes 3145732
  595.3 5.1 slice-start
  595.3 5.1 slice-start.1
  600.4 6.0 copy-start.1
  603.2 1.6 copy-start.4
where the time goes:
time: 610 us; the launch traced here: 606 us
  waiting for transfers between devices  369 us (60%)
  local copies, waits for them, and re-layouts  127 us (21%)
  matrix products  53.1 us (9%)
  other arithmetic  25.8 us (4%)
  starting transfers between devices  19.6 us (3%)
  loops' own time  11.7 us (2%)
    ppermute x3, waiting for transfers between devices, from_behind(): lax.ppermute(value, axis, [(source, source + steps) for source in range(i...  368 us
    dynamic_update_slice x16, local copies, waits for them, and re-layouts, local(): band_out = lax.map(attend_head, jnp.arange(H, dtype=jnp.int32))  74.9 us
    dot_general x16, matrix products, attend_head(): lax.dot_general(query_head, key_head, (((1,), (1,)), ((), ())), preferred...  25.6 us
    dot_general x16, matrix products, attend_head(): return jnp.dot(weights, value_head, preferred_element_type=jnp.float32)  21.2 us
    gather x1, local copies, waits for them, and re-layouts, local(): picked = arrived_flat[arrival].reshape(owners.shape + arrived.shape[-2:])  12.7 us
  transfers between devices with their start and end apart: 5, of which 4 were waited for; matrix products, arithmetic and copies ran while one was open for 25% of the time, Pallas kernels for 0%

commit v1 on v0

v1 whole, which is shorter than its diff:
```python
import functools
import math

import jax
import jax.numpy as jnp
from jax import lax
from jax.experimental import pallas as pl
from jax.experimental.pallas import tpu as pltpu
from jax.sharding import PartitionSpec as P

H = 16
QBLK = 128
MB = 64
RET = 8
DH = 128
BEHIND = 3
LOG2E = 1.4426950408889634
SCALE2 = LOG2E / math.sqrt(DH)
LOW = -1e30


def from_behind(value, axis, steps):
    count = lax.axis_size(axis)
    return lax.ppermute(value, axis, [(i, i + steps) for i in range(count - steps)])


def pick_kernel(req_ref, key_ref, value_ref, out_ref, sem, *, count):
    def step(i, carry):
        code = jnp.maximum(req_ref[i], 0)
        block = code // H
        col = pl.multiple_of((code % H) * DH, DH)
        pltpu.make_async_copy(key_ref.at[block, :, pl.ds(col, DH)], out_ref.at[i, 0], sem).start()
        pltpu.make_async_copy(value_ref.at[block, :, pl.ds(col, DH)], out_ref.at[i, 1], sem).start()
        return carry

    lax.fori_loop(0, count, step, 0)
    pltpu.make_async_copy(out_ref, out_ref, sem).wait()


def pick(requests, key_mem, value_mem):
    count = requests.shape[0]
    return pl.pallas_call(
        functools.partial(pick_kernel, count=count),
        out_shape=jax.ShapeDtypeStruct((count, 2, MB, DH), key_mem.dtype),
        in_specs=[
            pl.BlockSpec(memory_space=pltpu.SMEM),
            pl.BlockSpec(memory_space=pl.ANY),
            pl.BlockSpec(memory_space=pl.ANY),
        ],
        out_specs=pl.BlockSpec(memory_space=pl.ANY),
        scratch_shapes=[pltpu.SemaphoreType.DMA],
        name="pick",
    )(requests, key_mem, value_mem)


def softmax_dot(scores, value):
    top = jnp.max(scores, axis=1, keepdims=True)
    raised = jnp.exp2((scores - top) * SCALE2)
    total = jnp.sum(raised, axis=1, keepdims=True)
    out = jnp.dot(raised.astype(jnp.bfloat16), value, preferred_element_type=jnp.float32)
    return out / total


def scores_of(query, key):
    return lax.dot_general(query, key, (((1,), (1,)), ((), ())), preferred_element_type=jnp.float32)


def band_kernel(q_ref, k0, k1, k2, k3, v0, v1, v2, v3, out_ref):
    rows = q_ref.shape[0]
    position = lax.axis_index("blk")
    first = (BEHIND - position) * rows
    key = jnp.concatenate([k0[...], k1[...], k2[...], k3[...]], axis=0)
    value = jnp.concatenate([v0[...], v1[...], v2[...], v3[...]], axis=0)
    width = BEHIND * rows + QBLK
    for tile in range(rows // QBLK):
        base = tile * QBLK
        scores = scores_of(q_ref[base : base + QBLK, :], key[base : base + width, :])
        row = lax.broadcasted_iota(jnp.int32, scores.shape, 0)
        col = lax.broadcasted_iota(jnp.int32, scores.shape, 1)
        allowed = (col >= jnp.maximum(row, first - base)) & (col <= row + BEHIND * rows)
        scores = jnp.where(allowed, scores, LOW)
        out_ref[base : base + QBLK, :] = softmax_dot(scores, value[base : base + width, :])


def band(queries, key_parts, value_parts):
    rows, width = queries.shape
    spec = pl.BlockSpec((rows, DH), lambda h: (0, h))
    return pl.pallas_call(
        band_kernel,
        grid=(H,),
        out_shape=jax.ShapeDtypeStruct((rows, width), jnp.float32),
        in_specs=[spec] * 9,
        out_specs=spec,
        cost_estimate=pl.CostEstimate(
            flops=2 * 2 * rows * 1024 * width, bytes_accessed=rows * width * 24, transcendentals=rows * 1024 * H
        ),
        name="band",
    )(queries, *key_parts, *value_parts)


def memory_kernel(arrival_ref, gate_ref, q_ref, band_ref, *refs):
    blocks, out_ref = refs[:-1], refs[-1]
    share = gate_ref[pl.program_id(0)]
    for tile in range(len(blocks) // RET):
        part = blocks[tile * RET : (tile + 1) * RET]
        base = tile * QBLK
        key = jnp.concatenate([b[0, 0] for b in part], axis=0)
        value = jnp.concatenate([b[0, 1] for b in part], axis=0)
        memory_out = softmax_dot(scores_of(q_ref[base : base + QBLK, :], key), value)
        mixed = share * memory_out + (1.0 - share) * band_ref[base : base + QBLK, :]
        out_ref[base : base + QBLK, :] = mixed.astype(out_ref.dtype)


def memory(arrival, gate_share, queries, band_out, arrived):
    rows, width = queries.shape
    spec = pl.BlockSpec((rows, DH), lambda h, a, g: (0, h))

    def block_spec(tile, j):
        return pl.BlockSpec((1, 2, MB, DH), lambda h, a, g: (a[(tile * H + h) * RET + j], 0, 0, 0))

    picked = [block_spec(t, j) for t in range(rows // QBLK) for j in range(RET)]
    return pl.pallas_call(
        memory_kernel,
        grid_spec=pltpu.PrefetchScalarGridSpec(
            num_scalar_prefetch=2,
            grid=(H,),
            in_specs=[spec, spec] + picked,
            out_specs=spec,
        ),
        out_shape=jax.ShapeDtypeStruct((rows, width), jnp.bfloat16),
        name="memory",
    )(arrival, gate_share, queries, band_out, *([arrived] * len(picked)))


def plan_requests(target, local_code, peer_count, peer_slots):
    request_count = target.shape[0]
    order = jnp.arange(request_count, dtype=jnp.int32)
    same_target = (target[:, None] == target[None, :]) & (order[None, :] < order[:, None])
    slot_rank = jnp.sum(same_target.astype(jnp.int32), axis=1)
    arrival = target * peer_slots + slot_rank
    places = jnp.arange(peer_count * peer_slots, dtype=jnp.int32)
    hit = places[:, None] == arrival[None, :]
    requests = jnp.sum(jnp.where(hit, local_code[None, :], 0), axis=1)
    return requests.reshape(peer_count, peer_slots), arrival


def local(queries, keys, values, memory_keys, memory_values, owners, slots, gate_logit):
    target = owners.reshape(-1)
    head_flat = jnp.broadcast_to(jnp.arange(H, dtype=jnp.int32)[None, :, None], owners.shape).reshape(-1)
    peer_count = lax.axis_size("grp") * lax.axis_size("blk")
    capacity = max(2, 5 * target.shape[0] // (4 * peer_count))
    requests, arrival = plan_requests(target, slots.reshape(-1) * H + head_flat, peer_count, capacity)
    named = lax.all_to_all(requests, ("grp", "blk"), split_axis=0, concat_axis=0, tiled=True)
    picked = pick(named.reshape(-1), memory_keys, memory_values)
    picked = picked.reshape(peer_count, capacity, 2, MB, DH)
    arrived = lax.all_to_all(picked, ("grp", "blk"), split_axis=0, concat_axis=0, tiled=True)
    arrived = arrived.reshape(peer_count * capacity, 2, MB, DH)
    key_parts = [from_behind(keys, "blk", d) for d in range(BEHIND, 0, -1)] + [keys]
    value_parts = [from_behind(values, "blk", d) for d in range(BEHIND, 0, -1)] + [values]
    band_out = band(queries, key_parts, value_parts)
    return memory(arrival, jax.nn.sigmoid(gate_logit), queries, band_out, arrived)


def solution(mesh):
    rows = P(("grp", "blk"), None)
    blocks = P(("grp", "blk"), None, None)
    return jax.shard_map(
        local,
        mesh=mesh,
        in_specs=(rows, rows, rows, blocks, blocks, blocks, blocks, P()),
        out_specs=rows,
        check_vma=False,
    )
```

time: 610 us -> 750 us (1.23)
  Pallas kernels: 0 us -> 356 us
  local copies, waits for them, and re-layouts: 127 us -> 3.34 us
  matrix products: 53.1 us -> 0 us
  other arithmetic: 25.8 us -> 2.31 us
  waiting for transfers between devices: 369 us -> 353 us
  loops' own time: 11.7 us -> 0 us
  blocking collectives: 0 us -> 10.7 us
    pallas_call x0 -> x3, Pallas kernels: none -> 356 us  [the longest x1 319 us: pick(): pl.pallas_call(functools.partial(pick_kernel, count=count), out_shape=jax...]
    dynamic_update_slice x16 -> x0, local copies, waits for them, and re-layouts: 74.9 us -> none  [local(): band_out = lax.map(attend_head, jnp.arange(H, dtype=jnp.int32))]
    dot_general x34 -> x0, matrix products: 53.1 us -> none  [the longest x16 25.6 us: attend_head(): lax.dot_general(query_head, key_head, (((1,), (1,)), ((), ())), preferred...]
    gather x3 -> x0, local copies, waits for them, and re-layouts: 26 us -> none  [the longest x1 12.7 us: local(): picked = arrived_flat[arrival].reshape(owners.shape + arrived.shape[-2:])]
    concatenate x3 -> x0, other arithmetic: 17.2 us -> none  [the longest x1 10.7 us: pick_blocks(): return jnp.concatenate([picked_keys, picked_values], axis=-1)]
    ppermute x3 -> x6, waiting for transfers between devices: 368 us -> 353 us  [from_behind(): lax.ppermute(value, axis, [(i, i + steps) for i in range(count - steps)])]
    another operation x1 -> x0, loops' own time: 11.7 us -> none  [local(): band_out = lax.map(attend_head, jnp.arange(H, dtype=jnp.int32))]
    all_to_all x0 -> x1, blocking collectives: none -> 10.7 us  [local(): lax.all_to_all(requests, ('grp', 'blk'), split_axis=0, concat_axis=0, til...]
  transfers between devices with their start and end apart: 5 -> 7, of which waited for: 4 -> 5; matrix products, arithmetic and copies ran while one was open for 25% -> 0% of each run, Pallas kernels for 0% -> 2%
where the time goes in v1:
time: 750 us; the launch traced here: 748 us
  Pallas kernels  356 us (47%)
  waiting for transfers between devices  353 us (47%)
  starting transfers between devices  23.2 us (3%)
  blocking collectives  10.7 us (1%)
    ppermute x6, waiting for transfers between devices, from_behind(): lax.ppermute(value, axis, [(i, i + steps) for i in range(count - steps)])  353 us
    pallas_call x1, Pallas kernels, pick(): pl.pallas_call(functools.partial(pick_kernel, count=count), out_shape=jax...  319 us
    pallas_call x1, Pallas kernels, memory(): pl.pallas_call(memory_kernel, grid_spec=pltpu.PrefetchScalarGridSpec(num_...  18.2 us
    pallas_call x1, Pallas kernels, band(): pl.pallas_call(band_kernel, grid=(H,), out_shape=jax.ShapeDtypeStruct((ro...  18 us
    ppermute x6, starting transfers between devices, from_behind(): lax.ppermute(value, axis, [(i, i + steps) for i in range(count - steps)])  16.9 us
  transfers between devices with their start and end apart: 7, of which 5 were waited for; matrix products, arithmetic and copies ran while one was open for 0% of the time, Pallas kernels for 2%

profile of v1, /device:TPU:17, one launch (start us, length us, event | category | flops | bytes accessed | tf_op | source)
XLA Modules:
  0.0 748.1 jit_solution(11108230579424348888)
XLA Ops:
  0.0 0.8 copy.14
  0.9 0.2 convert_reduce_fusion
  1.1 0.7 iota_add_fusion
  2.2 10.7 %all_to_all.14 = s32[32,1,10]{2,1,0:T(1,128)S(1)} all-to-all(s32[32,1,10]{2,1,0:T(1,128)S(1)} %bitcast.4), channel_id=1, replica_groups=mesh['grp'=2,'blk'=16] {'grp','blk'}, dimensions={0} | all-to-all | bytes 2560 | tf_op jit(solution)/shard_map/all_to_all | solution.py:153
  12.9 0.5 broadcast.18
  13.4 0.7 reduce.3
  14.1 0.7 reshape.43.req_ref
  14.8 319.4 %pick.1 = bf16[320,2,64,128]{3,2,1,0:T(8,128)(2,1)} custom-call(s32[320]{0:T(512)} %reshape.43.req_ref, bf16[8,64,2048]{2,1,0:T(8,128)(2,1)} %key_ref.1, bf16[8,64,2048]{2,1,0:T(8,128)(2,1)} %value_ref.1), custom_call_target="tpu_custom_call" | custom-call | tf_op jit(solution)/shard_map/pick/pallas_call | solution.py:42
  334.3 6.2 all-to-all-start.1
  340.6 4.0 collective-permute-start
  344.6 3.1 collective-permute-start.1
  347.8 2.2 collective-permute-start.2
  350.0 3.7 collective-permute-start.3
  353.7 1.9 collective-permute-start.4
  355.7 245.4 %collective-permute-done.k0 = bf16[256,2048]{1,0:T(8,128)(2,1)S(1)} collective-permute-done((bf16[256,2048]{1,0:T(8,128)(2,1)S(1)}, bf16[256,2048]{1,0:T(8,128)(2,1)S(1)}, u32[]{:S(2)}, u32[]{:S(2)}) %collective-permute-start) | collective-permute-done | bytes 1048608 | tf_op jit(solution)/shard_map/ppermute | solution.py:24
  601.1 1.9 collective-permute-start.5
  603.0 0.6 add_divide_fusion.gate_ref
  603.6 17.4 %collective-permute-done.1.k1 = bf16[256,2048]{1,0:T(8,128)(2,1)S(1)} collective-permute-done((bf16[256,2048]{1,0:T(8,128)(2,1)S(1)}, bf16[256,2048]{1,0:T(8,128)(2,1)S(1)}, u32[]{:S(2)}, u32[]{:S(2)}) %collective-permute-start.1) | collective-permute-done | bytes 1048608 | tf_op jit(solution)/shard_map/ppermute | solution.py:24
  621.0 23.8 %collective-permute-done.2.k2 = bf16[256,2048]{1,0:T(8,128)(2,1)S(1)} collective-permute-done((bf16[256,2048]{1,0:T(8,128)(2,1)S(1)}, bf16[256,2048]{1,0:T(8,128)(2,1)S(1)}, u32[]{:S(2)}, u32[]{:S(2)}) %collective-permute-start.2) | collective-permute-done | bytes 1048608 | tf_op jit(solution)/shard_map/ppermute | solution.py:24
  644.8 22.0 %collective-permute-done.4.v1 = bf16[256,2048]{1,0:T(8,128)(2,1)S(1)} collective-permute-done((bf16[256,2048]{1,0:T(8,128)(2,1)S(1)}, bf16[256,2048]{1,0:T(8,128)(2,1)S(1)}, u32[]{:S(2)}, u32[]{:S(2)}) %collective-permute-start.4) | collective-permute-done | bytes 1048608 | tf_op jit(solution)/shard_map/ppermute | solution.py:24
  666.7 1.0 copy-done.6
  667.7 44.1 %collective-permute-done.5.v2 = bf16[256,2048]{1,0:T(8,128)(2,1)} collective-permute-done((bf16[256,2048]{1,0:T(8,128)(2,1)S(1)}, bf16[256,2048]{1,0:T(8,128)(2,1)}, u32[]{:S(2)}, u32[]{:S(2)}) %collective-permute-start.5) | collective-permute-done | bytes 1048608 | tf_op jit(solution)/shard_map/ppermute | solution.py:24
  711.8 18.0 %band.1.band_ref = f32[256,2048]{1,0:T(8,128)} custom-call(bf16[256,2048]{1,0:T(8,128)(2,1)} %q_ref.3, bf16[256,2048]{1,0:T(8,128)(2,1)} %copy-done.2, bf16[256,2048]{1,0:T(8,128)(2,1)} %copy-done.3, bf16[256,2048]{1,0:T(8,128)(2,1)} %copy-done.4, bf16[256,2048]{1,0:T(8,128)(2,1)} %k3.1, bf16[256,2048]{1,0:T(8,128)(2,1)} %copy-done.5, ...), custom_call_target="tpu_custom_call" | custom-call | flops 2147483648 | bytes 12582912 | tf_op jit(solution)/shard_map/band/pallas_call | solution.py:88
  729.8 18.2 %memory.1 = bf16[256,2048]{1,0:T(8,128)(2,1)} custom-call(s32[256]{0:T(256)} %copy-done.7, f32[16]{0:T(128)} %add_divide_fusion.gate_ref, bf16[256,2048]{1,0:T(8,128)(2,1)} %q_ref.3, f32[256,2048]{1,0:T(8,128)} %band.1.band_ref, ...), custom_call_target="tpu_custom_call" | custom-call | tf_op jit(solution)/shard_map/memory/pallas_call | solution.py:122
  (25 shorter events, 0.6 us)
Async XLA Ops:
  1.1 333.2 %copy-start.7 = (s32[256]{0:T(256)}, s32[256]{0:T(256)S(1)}, u32[]{:S(2)}) copy-start(s32[256]{0:T(256)S(1)} %multiply_add_fusion.arrival_ref) | copy-start | bytes 3076
  334.3 6.3 copy-start
  334.3 15.7 %copy-start.1 = (bf16[256,2048]{1,0:T(8,128)(2,1)S(1)}, bf16[256,2048]{1,0:T(8,128)(2,1)}, u32[]{:S(2)}) copy-start(bf16[256,2048]{1,0:T(8,128)(2,1)} %v3.1) | copy-start | bytes 3145732
  334.3 268.7 %copy-start.8 = (f32[16]{0:T(128)S(1)}, f32[16]{0:T(128)}, u32[]{:S(2)}) copy-start(f32[16]{0:T(128)} %param.15) | copy-start | bytes 196
  334.3 395.5 %all-to-all-start.1 = ((bf16[32,10,2,64,128]{4,3,2,1,0:T(8,128)(2,1)}), bf16[32,10,2,64,128]{4,3,2,1,0:T(8,128)(2,1)}, u32[]{:S(2)}, u32[]{:S(2)}) async-start(bf16[32,10,2,64,128]{4,3,2,1,0:T(8,128)(2,1)} %bitcast.3), calls=%async_computation.1 | async-start | bytes 20971520 | tf_op jit(solution)/shard_map/all_to_all | solution.py:156
  340.6 260.5 %collective-permute-start = (bf16[256,2048]{1,0:T(8,128)(2,1)S(1)}, bf16[256,2048]{1,0:T(8,128)(2,1)S(1)}, u32[]{:S(2)}, u32[]{:S(2)}) collective-permute-start(bf16[256,2048]{1,0:T(8,128)(2,1)S(1)} %copy-done), channel_id=1, source_target_pairs={{0,3},{1,4},{2,5},{3,6},{4,7},{5,8},{6,9},{7,10},{8,11},{9,12},{10... | collective-permute-start | bytes 3145736 | tf_op jit(solution)/shard_map/ppermute | solution.py:24
  344.6 276.4 %collective-permute-start.1 = (bf16[256,2048]{1,0:T(8,128)(2,1)S(1)}, bf16[256,2048]{1,0:T(8,128)(2,1)S(1)}, u32[]{:S(2)}, u32[]{:S(2)}) collective-permute-start(bf16[256,2048]{1,0:T(8,128)(2,1)S(1)} %copy-done), channel_id=1, source_target_pairs={{0,2},{1,3},{2,4},{3,5},{4,6},{5,7},{6,8},{7,9},{8,10},{9,11},{10,... | collective-permute-start | bytes 3145736 | tf_op jit(solution)/shard_map/ppermute | solution.py:24
  347.8 297.0 %collective-permute-start.2 = (bf16[256,2048]{1,0:T(8,128)(2,1)S(1)}, bf16[256,2048]{1,0:T(8,128)(2,1)S(1)}, u32[]{:S(2)}, u32[]{:S(2)}) collective-permute-start(bf16[256,2048]{1,0:T(8,128)(2,1)S(1)} %copy-done), channel_id=1, source_target_pairs={{0,1},{1,2},{2,3},{3,4},{4,5},{5,6},{6,7},{7,8},{8,9},{9,10},{10,1... | collective-permute-start | bytes 3145736 | tf_op jit(solution)/shard_map/ppermute | solution.py:24
  350.0 294.8 %collective-permute-start.3 = (bf16[256,2048]{1,0:T(8,128)(2,1)S(1)}, bf16[256,2048]{1,0:T(8,128)(2,1)S(1)}, u32[]{:S(2)}, u32[]{:S(2)}) collective-permute-start(bf16[256,2048]{1,0:T(8,128)(2,1)S(1)} %copy-done.1), channel_id=1, source_target_pairs={{0,3},{1,4},{2,5},{3,6},{4,7},{5,8},{6,9},{7,10},{8,11},{9,12},{10... | collective-permute-start | bytes 3145736 | tf_op jit(solution)/shard_map/ppermute | solution.py:24
  353.7 313.0 %collective-permute-start.4 = (bf16[256,2048]{1,0:T(8,128)(2,1)S(1)}, bf16[256,2048]{1,0:T(8,128)(2,1)S(1)}, u32[]{:S(2)}, u32[]{:S(2)}) collective-permute-start(bf16[256,2048]{1,0:T(8,128)(2,1)S(1)} %copy-done.1), channel_id=1, source_target_pairs={{0,2},{1,3},{2,4},{3,5},{4,6},{5,7},{6,8},{7,9},{8,10},{9,11},{10,... | collective-permute-start | bytes 3145736 | tf_op jit(solution)/shard_map/ppermute | solution.py:24
  601.1 110.7 %copy-start.2 = (bf16[256,2048]{1,0:T(8,128)(2,1)}, bf16[256,2048]{1,0:T(8,128)(2,1)S(1)}, u32[]{:S(2)}) copy-start(bf16[256,2048]{1,0:T(8,128)(2,1)S(1)} %collective-permute-done.k0) | copy-start | bytes 3145732
  601.1 110.7 %collective-permute-start.5 = (bf16[256,2048]{1,0:T(8,128)(2,1)S(1)}, bf16[256,2048]{1,0:T(8,128)(2,1)}, u32[]{:S(2)}, u32[]{:S(2)}) collective-permute-start(bf16[256,2048]{1,0:T(8,128)(2,1)S(1)} %copy-done.1), channel_id=1, source_target_pairs={{0,1},{1,2},{2,3},{3,4},{4,5},{5,6},{6,7},{7,8},{8,9},{9,10},{10,1... | collective-permute-start | bytes 3145736 | tf_op jit(solution)/shard_map/ppermute | solution.py:24
  621.0 45.7 %copy-start.3 = (bf16[256,2048]{1,0:T(8,128)(2,1)}, bf16[256,2048]{1,0:T(8,128)(2,1)S(1)}, u32[]{:S(2)}) copy-start(bf16[256,2048]{1,0:T(8,128)(2,1)S(1)} %collective-permute-done.1.k1) | copy-start | bytes 3145732
  644.7 22.0 %copy-start.4 = (bf16[256,2048]{1,0:T(8,128)(2,1)}, bf16[256,2048]{1,0:T(8,128)(2,1)S(1)}, u32[]{:S(2)}) copy-start(bf16[256,2048]{1,0:T(8,128)(2,1)S(1)} %collective-permute-done.2.k2) | copy-start | bytes 3145732
  644.8 22.0 %copy-start.5 = (bf16[256,2048]{1,0:T(8,128)(2,1)}, bf16[256,2048]{1,0:T(8,128)(2,1)S(1)}, u32[]{:S(2)}) copy-start(bf16[256,2048]{1,0:T(8,128)(2,1)S(1)} %collective-permute-done.3.v0) | copy-start | bytes 3145732
  666.7 1.0 copy-start.6

commit v2 on v1

--- a/solution.py
+++ b/solution.py
@@ -24,31 +24,44 @@
     return lax.ppermute(value, axis, [(i, i + steps) for i in range(count - steps)])
 
 
-def pick_kernel(req_ref, key_ref, value_ref, out_ref, sem, *, count):
-    def step(i, carry):
-        code = jnp.maximum(req_ref[i], 0)
-        block = code // H
-        col = pl.multiple_of((code % H) * DH, DH)
-        pltpu.make_async_copy(key_ref.at[block, :, pl.ds(col, DH)], out_ref.at[i, 0], sem).start()
-        pltpu.make_async_copy(value_ref.at[block, :, pl.ds(col, DH)], out_ref.at[i, 1], sem).start()
+def pick_kernel(req_ref, key_ref, value_ref, out_ref, held, sems, out_sem, *, peers, each):
+    def fetch(p, carry):
+        for r in range(each):
+            code = jnp.maximum(req_ref[p * each + r], 0)
+            block = code // H
+            col = pl.multiple_of((code % H) * DH, DH)
+            pltpu.make_async_copy(key_ref.at[block, :, pl.ds(col, DH)], held.at[p, r, 0], sems.at[p]).start()
+            pltpu.make_async_copy(value_ref.at[block, :, pl.ds(col, DH)], held.at[p, r, 1], sems.at[p]).start()
         return carry
 
-    lax.fori_loop(0, count, step, 0)
-    pltpu.make_async_copy(out_ref, out_ref, sem).wait()
+    def write(p, carry):
+        pltpu.make_async_copy(held.at[p], held.at[p], sems.at[p]).wait()
+        pltpu.make_async_copy(held.at[p], out_ref.at[p], out_sem).start()
+        return carry
+
+    lax.fori_loop(0, peers, fetch, 0)
+    lax.fori_loop(0, peers, write, 0)
+    pltpu.make_async_copy(held, out_ref, out_sem).wait()
 
 
-def pick(requests, key_mem, value_mem):
-    count = requests.shape[0]
+def pick(requests, key_mem, value_mem, peers):
+    each = requests.shape[0] // peers
+    shape = (peers, each, 2, MB, DH)
     return pl.pallas_call(
-        functools.partial(pick_kernel, count=count),
-        out_shape=jax.ShapeDtypeStruct((count, 2, MB, DH), key_mem.dtype),
+        functools.partial(pick_kernel, peers=peers, each=each),
+        out_shape=jax.ShapeDtypeStruct(shape, key_mem.dtype),
         in_specs=[
             pl.BlockSpec(memory_space=pltpu.SMEM),
             pl.BlockSpec(memory_space=pl.ANY),
             pl.BlockSpec(memory_space=pl.ANY),
         ],
         out_specs=pl.BlockSpec(memory_space=pl.ANY),
-        scratch_shapes=[pltpu.SemaphoreType.DMA],
+        scratch_shapes=[
+            pltpu.VMEM(shape, key_mem.dtype),
+            pltpu.SemaphoreType.DMA((peers,)),
+            pltpu.SemaphoreType.DMA,
+        ],
+        compiler_params=pltpu.CompilerParams(vmem_limit_bytes=32 << 20),
         name="pick",
     )(requests, key_mem, value_mem)
 
@@ -151,8 +164,7 @@
     capacity = max(2, 5 * target.shape[0] // (4 * peer_count))
     requests, arrival = plan_requests(target, slots.reshape(-1) * H + head_flat, peer_count, capacity)
     named = lax.all_to_all(requests, ("grp", "blk"), split_axis=0, concat_axis=0, tiled=True)
-    picked = pick(named.reshape(-1), memory_keys, memory_values)
-    picked = picked.reshape(peer_count, capacity, 2, MB, DH)
+    picked = pick(named.reshape(-1), memory_keys, memory_values, peer_count)
     arrived = lax.all_to_all(picked, ("grp", "blk"), split_axis=0, concat_axis=0, tiled=True)
     arrived = arrived.reshape(peer_count * capacity, 2, MB, DH)
     key_parts = [from_behind(keys, "blk", d) for d in range(BEHIND, 0, -1)] + [keys]

time: 750 us -> 448 us (0.60)
  Pallas kernels: 356 us -> 47.4 us
    pallas_call x1, Pallas kernels: 319 us -> 11.1 us  [pick(): pl.pallas_call(functools.partial(pick_kernel, peers=peers, each=each), ou...]
  transfers between devices with their start and end apart: 7 -> 7, of which waited for: 5 -> 5; matrix products, arithmetic and copies ran while one was open for 0% -> 0% of each run, Pallas kernels for 2% -> 4%
where the time goes in v2:
time: 448 us; the launch traced here: 446 us
  waiting for transfers between devices  353 us (79%)
  Pallas kernels  47.4 us (11%)
  starting transfers between devices  23.2 us (5%)
  blocking collectives  10.7 us (2%)
  local copies, waits for them, and re-layouts  9.74 us (2%)
    ppermute x6, waiting for transfers between devices, from_behind(): lax.ppermute(value, axis, [(i, i + steps) for i in range(count - steps)])  353 us
    pallas_call x1, Pallas kernels, memory(): pl.pallas_call(memory_kernel, grid_spec=pltpu.PrefetchScalarGridSpec(num_...  18.2 us
    pallas_call x1, Pallas kernels, band(): pl.pallas_call(band_kernel, grid=(H,), out_shape=jax.ShapeDtypeStruct((ro...  18 us
    ppermute x6, starting transfers between devices, from_behind(): lax.ppermute(value, axis, [(i, i + steps) for i in range(count - steps)])  16.9 us
    pallas_call x1, Pallas kernels, pick(): pl.pallas_call(functools.partial(pick_kernel, peers=peers, each=each), ou...  11.1 us
    all_to_all x1, blocking collectives, local(): lax.all_to_all(requests, ('grp', 'blk'), split_axis=0, concat_axis=0, til...  10.7 us
  transfers between devices with their start and end apart: 7, of which 5 were waited for; matrix products, arithmetic and copies ran while one was open for 0% of the time, Pallas kernels for 4%

profile of v2, /device:TPU:17, one launch (start us, length us, event | category | flops | bytes accessed | tf_op | source)
XLA Modules:
  0.0 446.1 jit_solution(9472670033152600829)
XLA Ops:
  0.0 0.8 copy.14
  1.1 0.7 iota_add_fusion
  2.2 10.7 %all_to_all.14 = s32[32,1,10]{2,1,0:T(1,128)S(1)} all-to-all(s32[32,1,10]{2,1,0:T(1,128)S(1)} %bitcast.2), channel_id=1, replica_groups=mesh['grp'=2,'blk'=16] {'grp','blk'}, dimensions={0} | all-to-all | bytes 2560 | tf_op jit(solution)/shard_map/all_to_all | solution.py:166
  13.4 0.7 reduce.3
  14.3 1.6 copy-done.1
  15.8 1.6 copy-done.2
  17.4 11.1 %pick.1 = bf16[32,10,2,64,128]{4,3,2,1,0:T(8,128)(2,1)S(1)} custom-call(s32[320]{0:T(512)S(1)} %reshape.40.req_ref, bf16[8,64,2048]{2,1,0:T(8,128)(2,1)S(1)} %copy-done.1, bf16[8,64,2048]{2,1,0:T(8,128)(2,1)S(1)} %copy-done.2), custom_call_target="tpu_custom_call" | custom-call | tf_op jit(solution)/shard_map/pick/pallas_call | solution.py:50
  28.6 3.8 copy-done
  32.4 6.2 %all-to-all-start.1 = ((bf16[32,10,2,64,128]{4,3,2,1,0:T(8,128)(2,1)}), bf16[32,10,2,64,128]{4,3,2,1,0:T(8,128)(2,1)}, u32[]{:S(2)}, u32[]{:S(2)}) async-start(bf16[32,10,2,64,128]{4,3,2,1,0:T(8,128)(2,1)} %copy-done), calls=%async_computation.1 | async-start | bytes 20971520 | tf_op jit(solution)/shard_map/all_to_all | solution.py:168
  38.7 4.0 collective-permute-start
  42.7 3.1 collective-permute-start.1
  45.8 2.2 collective-permute-start.2
  48.1 3.7 collective-permute-start.3
  51.8 1.9 collective-permute-start.4
  53.7 245.4 %collective-permute-done.k0 = bf16[256,2048]{1,0:T(8,128)(2,1)S(1)} collective-permute-done((bf16[256,2048]{1,0:T(8,128)(2,1)S(1)}, bf16[256,2048]{1,0:T(8,128)(2,1)S(1)}, u32[]{:S(2)}, u32[]{:S(2)}) %collective-permute-start) | collective-permute-done | bytes 1048608 | tf_op jit(solution)/shard_map/ppermute | solution.py:24
  299.2 1.9 collective-permute-start.5
  301.1 0.6 add_divide_fusion.gate_ref
  301.7 17.4 %collective-permute-done.1.k1 = bf16[256,2048]{1,0:T(8,128)(2,1)S(1)} collective-permute-done((bf16[256,2048]{1,0:T(8,128)(2,1)S(1)}, bf16[256,2048]{1,0:T(8,128)(2,1)S(1)}, u32[]{:S(2)}, u32[]{:S(2)}) %collective-permute-start.1) | collective-permute-done | bytes 1048608 | tf_op jit(solution)/shard_map/ppermute | solution.py:24
  319.1 23.8 %collective-permute-done.2.k2 = bf16[256,2048]{1,0:T(8,128)(2,1)S(1)} collective-permute-done((bf16[256,2048]{1,0:T(8,128)(2,1)S(1)}, bf16[256,2048]{1,0:T(8,128)(2,1)S(1)}, u32[]{:S(2)}, u32[]{:S(2)}) %collective-permute-start.2) | collective-permute-done | bytes 1048608 | tf_op jit(solution)/shard_map/ppermute | solution.py:24
  342.8 22.0 %collective-permute-done.4.v1 = bf16[256,2048]{1,0:T(8,128)(2,1)S(1)} collective-permute-done((bf16[256,2048]{1,0:T(8,128)(2,1)S(1)}, bf16[256,2048]{1,0:T(8,128)(2,1)S(1)}, u32[]{:S(2)}, u32[]{:S(2)}) %collective-permute-start.4) | collective-permute-done | bytes 1048608 | tf_op jit(solution)/shard_map/ppermute | solution.py:24
  364.8 1.0 copy-done.9
  365.8 44.1 %collective-permute-done.5.v2 = bf16[256,2048]{1,0:T(8,128)(2,1)} collective-permute-done((bf16[256,2048]{1,0:T(8,128)(2,1)S(1)}, bf16[256,2048]{1,0:T(8,128)(2,1)}, u32[]{:S(2)}, u32[]{:S(2)}) %collective-permute-start.5) | collective-permute-done | bytes 1048608 | tf_op jit(solution)/shard_map/ppermute | solution.py:24
  409.9 18.0 %band.1.band_ref = f32[256,2048]{1,0:T(8,128)} custom-call(bf16[256,2048]{1,0:T(8,128)(2,1)} %q_ref.3, bf16[256,2048]{1,0:T(8,128)(2,1)} %copy-done.5, bf16[256,2048]{1,0:T(8,128)(2,1)} %copy-done.6, bf16[256,2048]{1,0:T(8,128)(2,1)} %copy-done.7, bf16[256,2048]{1,0:T(8,128)(2,1)} %k3.1, bf16[256,2048]{1,0:T(8,128)(2,1)} %copy-done.8, ...), custom_call_target="tpu_custom_call" | custom-call | flops 2147483648 | bytes 12582912 | tf_op jit(solution)/shard_map/band/pallas_call | solution.py:101
  427.9 18.2 %memory.1 = bf16[256,2048]{1,0:T(8,128)(2,1)} custom-call(s32[256]{0:T(256)} %copy-done.10, f32[16]{0:T(128)} %add_divide_fusion.gate_ref, bf16[256,2048]{1,0:T(8,128)(2,1)} %q_ref.3, f32[256,2048]{1,0:T(8,128)} %band.1.band_ref, ...), custom_call_target="tpu_custom_call" | custom-call | tf_op jit(solution)/shard_map/memory/pallas_call | solution.py:135
  (31 shorter events, 1.4 us)
Async XLA Ops:
  1.1 27.5 %copy-start.10 = (s32[256]{0:T(256)}, s32[256]{0:T(256)S(1)}, u32[]{:S(2)}) copy-start(s32[256]{0:T(256)S(1)} %multiply_add_fusion.arrival_ref) | copy-start | bytes 3076
  14.2 1.6 copy-start.1
  15.8 1.6 copy-start.2
  28.6 3.8 copy-start
  32.4 6.2 %copy-start.3 = (bf16[256,2048]{1,0:T(8,128)(2,1)S(1)}, bf16[256,2048]{1,0:T(8,128)(2,1)}, u32[]{:S(2)}) copy-start(bf16[256,2048]{1,0:T(8,128)(2,1)} %k3.1) | copy-start | bytes 3145732
  32.4 15.6 %copy-start.4 = (bf16[256,2048]{1,0:T(8,128)(2,1)S(1)}, bf16[256,2048]{1,0:T(8,128)(2,1)}, u32[]{:S(2)}) copy-start(bf16[256,2048]{1,0:T(8,128)(2,1)} %v3.1) | copy-start | bytes 3145732
  32.4 268.7 %copy-start.11 = (f32[16]{0:T(128)S(1)}, f32[16]{0:T(128)}, u32[]{:S(2)}) copy-start(f32[16]{0:T(128)} %param.15) | copy-start | bytes 196
  32.4 395.5 %all-to-all-start.1 = ((bf16[32,10,2,64,128]{4,3,2,1,0:T(8,128)(2,1)}), bf16[32,10,2,64,128]{4,3,2,1,0:T(8,128)(2,1)}, u32[]{:S(2)}, u32[]{:S(2)}) async-start(bf16[32,10,2,64,128]{4,3,2,1,0:T(8,128)(2,1)} %copy-done), calls=%async_computation.1 | async-start | bytes 20971520 | tf_op jit(solution)/shard_map/all_to_all | solution.py:168
  38.7 260.5 %collective-permute-start = (bf16[256,2048]{1,0:T(8,128)(2,1)S(1)}, bf16[256,2048]{1,0:T(8,128)(2,1)S(1)}, u32[]{:S(2)}, u32[]{:S(2)}) collective-permute-start(bf16[256,2048]{1,0:T(8,128)(2,1)S(1)} %copy-done.3), channel_id=1, source_target_pairs={{0,3},{1,4},{2,5},{3,6},{4,7},{5,8},{6,9},{7,10},{8,11},{9,12},{10... | collective-permute-start | bytes 3145736 | tf_op jit(solution)/shard_map/ppermute | solution.py:24
  42.7 276.4 %collective-permute-start.1 = (bf16[256,2048]{1,0:T(8,128)(2,1)S(1)}, bf16[256,2048]{1,0:T(8,128)(2,1)S(1)}, u32[]{:S(2)}, u32[]{:S(2)}) collective-permute-start(bf16[256,2048]{1,0:T(8,128)(2,1)S(1)} %copy-done.3), channel_id=1, source_target_pairs={{0,2},{1,3},{2,4},{3,5},{4,6},{5,7},{6,8},{7,9},{8,10},{9,11},{10,... | collective-permute-start | bytes 3145736 | tf_op jit(solution)/shard_map/ppermute | solution.py:24
  45.8 297.0 %collective-permute-start.2 = (bf16[256,2048]{1,0:T(8,128)(2,1)S(1)}, bf16[256,2048]{1,0:T(8,128)(2,1)S(1)}, u32[]{:S(2)}, u32[]{:S(2)}) collective-permute-start(bf16[256,2048]{1,0:T(8,128)(2,1)S(1)} %copy-done.3), channel_id=1, source_target_pairs={{0,1},{1,2},{2,3},{3,4},{4,5},{5,6},{6,7},{7,8},{8,9},{9,10},{10,1... | collective-permute-start | bytes 3145736 | tf_op jit(solution)/shard_map/ppermute | solution.py:24
  48.1 294.8 %collective-permute-start.3 = (bf16[256,2048]{1,0:T(8,128)(2,1)S(1)}, bf16[256,2048]{1,0:T(8,128)(2,1)S(1)}, u32[]{:S(2)}, u32[]{:S(2)}) collective-permute-start(bf16[256,2048]{1,0:T(8,128)(2,1)S(1)} %copy-done.4), channel_id=1, source_target_pairs={{0,3},{1,4},{2,5},{3,6},{4,7},{5,8},{6,9},{7,10},{8,11},{9,12},{10... | collective-permute-start | bytes 3145736 | tf_op jit(solution)/shard_map/ppermute | solution.py:24
  51.8 313.0 %collective-permute-start.4 = (bf16[256,2048]{1,0:T(8,128)(2,1)S(1)}, bf16[256,2048]{1,0:T(8,128)(2,1)S(1)}, u32[]{:S(2)}, u32[]{:S(2)}) collective-permute-start(bf16[256,2048]{1,0:T(8,128)(2,1)S(1)} %copy-done.4), channel_id=1, source_target_pairs={{0,2},{1,3},{2,4},{3,5},{4,6},{5,7},{6,8},{7,9},{8,10},{9,11},{10,... | collective-permute-start | bytes 3145736 | tf_op jit(solution)/shard_map/ppermute | solution.py:24
  299.2 110.7 %copy-start.5 = (bf16[256,2048]{1,0:T(8,128)(2,1)}, bf16[256,2048]{1,0:T(8,128)(2,1)S(1)}, u32[]{:S(2)}) copy-start(bf16[256,2048]{1,0:T(8,128)(2,1)S(1)} %collective-permute-done.k0) | copy-start | bytes 3145732
  299.2 110.7 %collective-permute-start.5 = (bf16[256,2048]{1,0:T(8,128)(2,1)S(1)}, bf16[256,2048]{1,0:T(8,128)(2,1)}, u32[]{:S(2)}, u32[]{:S(2)}) collective-permute-start(bf16[256,2048]{1,0:T(8,128)(2,1)S(1)} %copy-done.4), channel_id=1, source_target_pairs={{0,1},{1,2},{2,3},{3,4},{4,5},{5,6},{6,7},{7,8},{8,9},{9,10},{10,1... | collective-permute-start | bytes 3145736 | tf_op jit(solution)/shard_map/ppermute | solution.py:24
  319.1 45.7 %copy-start.6 = (bf16[256,2048]{1,0:T(8,128)(2,1)}, bf16[256,2048]{1,0:T(8,128)(2,1)S(1)}, u32[]{:S(2)}) copy-start(bf16[256,2048]{1,0:T(8,128)(2,1)S(1)} %collective-permute-done.1.k1) | copy-start | bytes 3145732
  342.8 22.0 %copy-start.7 = (bf16[256,2048]{1,0:T(8,128)(2,1)}, bf16[256,2048]{1,0:T(8,128)(2,1)S(1)}, u32[]{:S(2)}) copy-start(bf16[256,2048]{1,0:T(8,128)(2,1)S(1)} %collective-permute-done.2.k2) | copy-start | bytes 3145732
  342.8 22.0 %copy-start.8 = (bf16[256,2048]{1,0:T(8,128)(2,1)}, bf16[256,2048]{1,0:T(8,128)(2,1)S(1)}, u32[]{:S(2)}) copy-start(bf16[256,2048]{1,0:T(8,128)(2,1)S(1)} %collective-permute-done.3.v0) | copy-start | bytes 3145732
  364.8 1.0 copy-start.9

commit v3 on v2

--- a/solution.py
+++ b/solution.py
@@ -14,6 +14,7 @@
 RET = 8
 DH = 128
 BEHIND = 3
+GROUP = BEHIND + 1
 LOG2E = 1.4426950408889634
 SCALE2 = LOG2E / math.sqrt(DH)
 LOW = -1e30
@@ -61,7 +62,7 @@
             pltpu.SemaphoreType.DMA((peers,)),
             pltpu.SemaphoreType.DMA,
         ],
-        compiler_params=pltpu.CompilerParams(vmem_limit_bytes=32 << 20),
+        compiler_params=pltpu.CompilerParams(vmem_limit_bytes=56 << 20),
         name="pick",
     )(requests, key_mem, value_mem)
 
@@ -78,37 +79,94 @@
     return lax.dot_general(query, key, (((1,), (1,)), ((), ())), preferred_element_type=jnp.float32)
 
 
-def band_kernel(q_ref, k0, k1, k2, k3, v0, v1, v2, v3, out_ref):
-    rows = q_ref.shape[0]
-    position = lax.axis_index("blk")
-    first = (BEHIND - position) * rows
-    key = jnp.concatenate([k0[...], k1[...], k2[...], k3[...]], axis=0)
-    value = jnp.concatenate([v0[...], v1[...], v2[...], v3[...]], axis=0)
-    width = BEHIND * rows + QBLK
-    for tile in range(rows // QBLK):
+def band_kernel(q_ref, key_ref, value_ref, key_before, value_before, out_ref):
+    rows = q_ref.shape[2]
+    behind = BEHIND * rows
+    place = lax.axis_index("blk")
+    first = jnp.where(place < GROUP, behind, 0)
+    key = jnp.concatenate([key_before[...].reshape(behind, DH), key_ref[...].reshape(GROUP * rows, DH)], axis=0)
+    value = jnp.concatenate([value_before[...].reshape(behind, DH), value_ref[...].reshape(GROUP * rows, DH)], axis=0)
+    width = behind + QBLK
+    for tile in range(GROUP * rows // QBLK):
         base = tile * QBLK
-        scores = scores_of(q_ref[base : base + QBLK, :], key[base : base + width, :])
+        member, start = divmod(base, rows)
+        scores = scores_of(q_ref[member, 0, start : start + QBLK, :], key[base : base + width, :])
         row = lax.broadcasted_iota(jnp.int32, scores.shape, 0)
         col = lax.broadcasted_iota(jnp.int32, scores.shape, 1)
-        allowed = (col >= jnp.maximum(row, first - base)) & (col <= row + BEHIND * rows)
+        allowed = (col >= jnp.maximum(row, first - base)) & (col <= row + behind)
         scores = jnp.where(allowed, scores, LOW)
-        out_ref[base : base + QBLK, :] = softmax_dot(scores, value[base : base + width, :])
-
-
-def band(queries, key_parts, value_parts):
+        result = softmax_dot(scores, value[base : base + width, :])
+        shift = (member - place % GROUP + GROUP) % GROUP
+        out_ref[shift, start : start + QBLK, :] = result.astype(out_ref.dtype)
+
+
+def band(gathered, before):
+    members, _, rows, width = gathered.shape
+
+    def spec(which):
+        return pl.BlockSpec((members, 1, rows, DH), lambda h: (0, which, 0, h))
+
+    def spec_before(which):
+        return pl.BlockSpec((BEHIND, 1, rows, DH), lambda h: (0, which, 0, h))
+
+    return pl.pallas_call(
+        band_kernel,
+        grid=(width // DH,),
+        out_shape=jax.ShapeDtypeStruct((members, rows, width), jnp.bfloat16),
+        in_specs=[spec(0), spec(1), spec(2), spec_before(0), spec_before(1)],
+        out_specs=pl.BlockSpec((members, rows, DH), lambda h: (0, 0, h)),
+        cost_estimate=pl.CostEstimate(
+            flops=2 * 2 * members * rows * 1024 * width,
+            bytes_accessed=members * rows * width * 14,
+            transcendentals=members * rows * 1024 * width // DH,
+        ),
+        compiler_params=pltpu.CompilerParams(vmem_limit_bytes=56 << 20),
+        name="band",
+    )(gathered, gathered, gathered, before, before)
+
+
+def pack_kernel(q_ref, k_ref, v_ref, out_ref):
+    out_ref[0, 0] = q_ref[...]
+    out_ref[0, 1] = k_ref[...]
+    out_ref[0, 2] = v_ref[...]
+
+
+def pack(queries, keys, values):
     rows, width = queries.shape
-    spec = pl.BlockSpec((rows, DH), lambda h: (0, h))
-    return pl.pallas_call(
-        band_kernel,
-        grid=(H,),
-        out_shape=jax.ShapeDtypeStruct((rows, width), jnp.float32),
-        in_specs=[spec] * 9,
-        out_specs=spec,
-        cost_estimate=pl.CostEstimate(
-            flops=2 * 2 * rows * 1024 * width, bytes_accessed=rows * width * 24, transcendentals=rows * 1024 * H
-        ),
-        name="band",
-    )(queries, *key_parts, *value_parts)
+    part = width // GROUP
+    spec = pl.BlockSpec((rows, part), lambda g: (0, g))
+    return pl.pallas_call(
+        pack_kernel,
+        grid=(GROUP,),
+        out_shape=jax.ShapeDtypeStruct((GROUP, 3, rows, part), queries.dtype),
+        in_specs=[spec] * 3,
+        out_specs=pl.BlockSpec((1, 3, rows, part), lambda g: (g, 0, 0, 0)),
+        compiler_params=pltpu.CompilerParams(vmem_limit_bytes=56 << 20),
+        name="pack",
+    )(queries, keys, values)
+
+
+def gather_heads(queries, keys, values):
+    count = lax.axis_size("blk")
+    groups = [[g + i for i in range(GROUP)] for g in range(0, count, GROUP)]
+    gathered = lax.all_to_all(
+        pack(queries, keys, values),
+        "blk",
+        split_axis=0,
+        concat_axis=0,
+        axis_index_groups=groups,
+        tiled=True,
+    )
+    return gathered, from_behind(gathered[GROUP - BEHIND :, 1:], "blk", GROUP)
+
+
+def return_rows(parts):
+    count = lax.axis_size("blk")
+    back = [parts[0]]
+    for shift in range(1, GROUP):
+        pairs = [(i, i // GROUP * GROUP + (i + shift) % GROUP) for i in range(count)]
+        back.append(lax.ppermute(parts[shift], "blk", pairs))
+    return jnp.stack(back)
 
 
 def memory_kernel(arrival_ref, gate_ref, q_ref, band_ref, *refs):
@@ -120,13 +178,17 @@
         key = jnp.concatenate([b[0, 0] for b in part], axis=0)
         value = jnp.concatenate([b[0, 1] for b in part], axis=0)
         memory_out = softmax_dot(scores_of(q_ref[base : base + QBLK, :], key), value)
-        mixed = share * memory_out + (1.0 - share) * band_ref[base : base + QBLK, :]
+        mixed = share * memory_out + (1.0 - share) * band_ref[0, base : base + QBLK, :].astype(jnp.float32)
         out_ref[base : base + QBLK, :] = mixed.astype(out_ref.dtype)
 
 
 def memory(arrival, gate_share, queries, band_out, arrived):
     rows, width = queries.shape
     spec = pl.BlockSpec((rows, DH), lambda h, a, g: (0, h))
+
+    each = H // GROUP
+    last = arrival.shape[0] - 1
+    band_spec = pl.BlockSpec((1, rows, DH), lambda h, a, g: ((a[last] - h // each + GROUP) % GROUP, 0, h % each))
 
     def block_spec(tile, j):
         return pl.BlockSpec((1, 2, MB, DH), lambda h, a, g: (a[(tile * H + h) * RET + j], 0, 0, 0))
@@ -137,7 +199,7 @@
         grid_spec=pltpu.PrefetchScalarGridSpec(
             num_scalar_prefetch=2,
             grid=(H,),
-            in_specs=[spec, spec] + picked,
+            in_specs=[spec, band_spec] + picked,
             out_specs=spec,
         ),
         out_shape=jax.ShapeDtypeStruct((rows, width), jnp.bfloat16),
@@ -164,12 +226,14 @@
     capacity = max(2, 5 * target.shape[0] // (4 * peer_count))
     requests, arrival = plan_requests(target, slots.reshape(-1) * H + head_flat, peer_count, capacity)
     named = lax.all_to_all(requests, ("grp", "blk"), split_axis=0, concat_axis=0, tiled=True)
+    gathered, before = gather_heads(queries, keys, values)
+    named, before = lax.optimization_barrier((named, before))
     picked = pick(named.reshape(-1), memory_keys, memory_values, peer_count)
     arrived = lax.all_to_all(picked, ("grp", "blk"), split_axis=0, concat_axis=0, tiled=True)
     arrived = arrived.reshape(peer_count * capacity, 2, MB, DH)
-    key_parts = [from_behind(keys, "blk", d) for d in range(BEHIND, 0, -1)] + [keys]
-    value_parts = [from_behind(values, "blk", d) for d in range(BEHIND, 0, -1)] + [values]
-    band_out = band(queries, key_parts, value_parts)
+    band_out = return_rows(band(gathered, before))
+    member = lax.axis_index("blk") % GROUP
+    arrival = jnp.concatenate([arrival, member[None].astype(jnp.int32)])
     return memory(arrival, jax.nn.sigmoid(gate_logit), queries, band_out, arrived)
 
 

time: 448 us -> 366 us (0.82)
  waiting for transfers between devices: 353 us -> 217 us
  blocking collectives: 10.7 us -> 74.6 us
  starting transfers between devices: 23.2 us -> 12 us
  local copies, waits for them, and re-layouts: 9.74 us -> 3.72 us
  Pallas kernels: 47.4 us -> 52.1 us
    ppermute x6 -> x1, waiting for transfers between devices: 353 us -> 0.01 us  [from_behind(): lax.ppermute(value, axis, [(i, i + steps) for i in range(count - steps)])]
    all_to_all x1, waiting for transfers between devices: 0.01 us -> 159 us  [local(): lax.all_to_all(picked, ('grp', 'blk'), split_axis=0, concat_axis=0, tiled...]
    ppermute x0 -> x3, waiting for transfers between devices: none -> 57.4 us  [return_rows(): back.append(lax.ppermute(parts[shift], 'blk', pairs))]
    all_to_all x0 -> x1, blocking collectives: none -> 39.2 us  [gather_heads(): lax.all_to_all(pack(queries, keys, values), 'blk', split_axis=0, concat_a...]
    all_to_all x1, blocking collectives: 10.7 us -> 35.4 us  [local(): lax.all_to_all(requests, ('grp', 'blk'), split_axis=0, concat_axis=0, til...]
    ppermute x6 -> x1, starting transfers between devices: 16.9 us -> 3.19 us  [from_behind(): lax.ppermute(value, axis, [(i, i + steps) for i in range(count - steps)])]
    unnamed x25 -> x9, local copies, waits for them, and re-layouts: 8.77 us -> 0.09 us
    pallas_call x1 -> x2, Pallas kernels: 18 us -> 18.4 us  [the longest x1 14.3 us: band(): pl.pallas_call(band_kernel, grid=(width // DH,), out_shape=jax.ShapeDtype...]
  transfers between devices with their start and end apart: 7 -> 5, of which waited for: 5 -> 3; matrix products, arithmetic and copies ran while one was open for 0% -> 1% of each run, Pallas kernels for 4% -> 4%
where the time goes in v3:
time: 366 us; the launch traced here: 362 us
  waiting for transfers between devices  217 us (59%)
  blocking collectives  74.6 us (20%)
  Pallas kernels  52.1 us (14%)
  starting transfers between devices  12 us (3%)
  local copies, waits for them, and re-layouts  3.72 us (1%)
    all_to_all x1, waiting for transfers between devices, local(): lax.all_to_all(picked, ('grp', 'blk'), split_axis=0, concat_axis=0, tiled...  159 us
    ppermute x3, waiting for transfers between devices, return_rows(): back.append(lax.ppermute(parts[shift], 'blk', pairs))  57.4 us
    all_to_all x1, blocking collectives, gather_heads(): lax.all_to_all(pack(queries, keys, values), 'blk', split_axis=0, concat_a...  39.2 us
    all_to_all x1, blocking collectives, local(): lax.all_to_all(requests, ('grp', 'blk'), split_axis=0, concat_axis=0, til...  35.4 us
    pallas_call x1, Pallas kernels, memory(): pl.pallas_call(memory_kernel, grid_spec=pltpu.PrefetchScalarGridSpec(num_...  18.8 us
    pallas_call x1, Pallas kernels, pick(): pl.pallas_call(functools.partial(pick_kernel, peers=peers, each=each), ou...  14.9 us
    pallas_call x1, Pallas kernels, band(): pl.pallas_call(band_kernel, grid=(width // DH,), out_shape=jax.ShapeDtype...  14.3 us
  transfers between devices with their start and end apart: 5, of which 3 were waited for; matrix products, arithmetic and copies ran while one was open for 1% of the time, Pallas kernels for 4%

profile of v3, /device:TPU:17, one launch (start us, length us, event | category | flops | bytes accessed | tf_op | source)
XLA Modules:
  0.0 361.6 jit_solution(6796655439556730493)
XLA Ops:
  0.0 4.2 %pack.1 = bf16[4,3,256,512]{3,2,1,0:T(8,128)(2,1)} custom-call(bf16[256,2048]{1,0:T(8,128)(2,1)} %q_ref.3, bf16[256,2048]{1,0:T(8,128)(2,1)} %k_ref.1, bf16[256,2048]{1,0:T(8,128)(2,1)} %v_ref.1), custom_call_target="tpu_custom_call" | custom-call | tf_op jit(solution)/shard_map/pack/pallas_call | solution.py:138
  4.2 39.2 %all_to_all.22.q_ref.key_ref.value_ref = bf16[4,3,256,512]{3,2,1,0:T(8,128)(2,1)S(1)} all-to-all(bf16[4,3,256,512]{3,2,1,0:T(8,128)(2,1)} %pack.1), channel_id=1, replica_groups={{0,1,2,3},{4,5,6,7},{8,9,10,11},{12,13,14,15},{16,17,18,19},{20,21,22,2..., dimensions={0} | all-to-all | bytes 6291456 | tf_op jit(solution)/shard_map/all_to_all | solution.py:152
  43.4 1.3 slice.20
  44.7 3.2 collective-permute-start
  48.0 0.1 reshape.38
  48.3 0.2 convert_reduce_fusion
  48.5 0.2 select_reduce_fusion
  48.6 0.1 all_to_all.15
  48.7 35.4 %all_to_all.23 = s32[32,1,10]{2,1,0:T(1,128)S(1)} all-to-all(s32[32,1,10]{2,1,0:T(1,128)S(1)} %bitcast.17), channel_id=1, replica_groups=mesh['grp'=2,'blk'=16] {'grp','blk'}, dimensions={0} | all-to-all | bytes 2560 | tf_op jit(solution)/shard_map/all_to_all | solution.py:228
  84.2 0.7 reshape.39.req_ref
  84.9 14.9 %pick.1 = bf16[32,10,2,64,128]{4,3,2,1,0:T(8,128)(2,1)} custom-call(s32[320]{0:T(512)} %reshape.39.req_ref, bf16[8,64,2048]{2,1,0:T(8,128)(2,1)} %key_ref.1, bf16[8,64,2048]{2,1,0:T(8,128)(2,1)} %value_ref.1), custom_call_target="tpu_custom_call" | custom-call | tf_op jit(solution)/shard_map/pick/pallas_call | solution.py:51
  99.8 5.2 %all-to-all-start.2 = ((bf16[32,10,2,64,128]{4,3,2,1,0:T(8,128)(2,1)}), bf16[32,10,2,64,128]{4,3,2,1,0:T(8,128)(2,1)}, u32[]{:S(2)}, u32[]{:S(2)}) async-start(bf16[32,10,2,64,128]{4,3,2,1,0:T(8,128)(2,1)} %pick.1), calls=%async_computation.2 | async-start | bytes 20971520 | tf_op jit(solution)/shard_map/all_to_all | solution.py:232
  105.0 14.3 %band.1 = bf16[4,256,512]{2,1,0:T(8,128)(2,1)} custom-call(bf16[4,3,256,512]{3,2,1,0:T(8,128)(2,1)} %copy-done, bf16[4,3,256,512]{3,2,1,0:T(8,128)(2,1)} %copy-done, bf16[4,3,256,512]{3,2,1,0:T(8,128)(2,1)} %copy-done, bf16[3,2,256,512]{3,2,1,0:T(8,128)(2,1)} %collective-permute-done.key_before.value_before, ...), custom_call_target="tpu_custom_call" | custom-call | flops 2147483648 | bytes 7340032 | tf_op jit(solution)/shard_map/band/pallas_call | solution.py:112
  119.2 1.3 fusion.1
  120.5 1.2 collective-permute-start.1
  121.7 1.2 collective-permute-start.2
  122.9 1.2 collective-permute-start.3
  124.1 0.6 pad_add_fusion.arrival_ref
  124.7 0.5 add_divide_fusion.gate_ref
  125.2 48.6 %collective-permute-done.1 = bf16[256,512]{1,0:T(8,128)(2,1)S(1)} collective-permute-done((bf16[256,512]{1,0:T(8,128)(2,1)S(1)}, bf16[256,512]{1,0:T(8,128)(2,1)S(1)}, u32[]{:S(2)}, u32[]{:S(2)}) %collective-permute-start.1) | collective-permute-done | bytes 262176 | tf_op jit(solution)/shard_map/ppermute | solution.py:168
  173.8 8.8 %collective-permute-done.3 = bf16[256,512]{1,0:T(8,128)(2,1)S(1)} collective-permute-done((bf16[256,512]{1,0:T(8,128)(2,1)S(1)}, bf16[256,512]{1,0:T(8,128)(2,1)S(1)}, u32[]{:S(2)}, u32[]{:S(2)}) %collective-permute-start.3) | collective-permute-done | bytes 262176 | tf_op jit(solution)/shard_map/ppermute | solution.py:168
  182.7 1.1 pad_maximum_fusion.band_ref
  183.8 159.1 %all-to-all-done.2 = bf16[32,10,2,64,128]{4,3,2,1,0:T(8,128)(2,1)} async-done(((bf16[32,10,2,64,128]{4,3,2,1,0:T(8,128)(2,1)}), bf16[32,10,2,64,128]{4,3,2,1,0:T(8,128)(2,1)}, u32[]{:S(2)}, u32[]{:S(2)}) %all-to-all-start.2) | async-done | bytes 10485792 | tf_op jit(solution)/shard_map/all_to_all | solution.py:232
  342.8 18.8 %memory.1 = bf16[256,2048]{1,0:T(8,128)(2,1)} custom-call(s32[257]{0:T(512)} %pad_add_fusion.arrival_ref, f32[16]{0:T(128)} %add_divide_fusion.gate_ref, bf16[256,2048]{1,0:T(8,128)(2,1)} %q_ref.3, bf16[4,256,512]{2,1,0:T(8,128)(2,1)} %pad_maximum_fusion.band_ref, ...), custom_call_target="tpu_custom_call" | custom-call | tf_op jit(solution)/shard_map/memory/pallas_call | solution.py:197
  (15 shorter events, 0.3 us)
Async XLA Ops:
  4.2 43.7 %copy-start.1 = (s32[2,16,8]{1,2,0:T(8,128)S(1)}, s32[2,16,8]{1,2,0:T(8,128)}, u32[]{:S(2)}) copy-start(s32[2,16,8]{1,2,0:T(8,128)} %param.13) | copy-start | bytes 3076
  43.4 56.4 %copy-start = (bf16[4,3,256,512]{3,2,1,0:T(8,128)(2,1)}, bf16[4,3,256,512]{3,2,1,0:T(8,128)(2,1)S(1)}, u32[]{:S(2)}) copy-start(bf16[4,3,256,512]{3,2,1,0:T(8,128)(2,1)S(1)} %all_to_all.22.q_ref.key_ref.value_ref) | copy-start | bytes 9437188
  43.4 4.7 %copy-start.2 = (s32[2,16,8]{1,2,0:T(8,128)S(1)}, s32[2,16,8]{1,2,0:T(8,128)}, u32[]{:S(2)}) copy-start(s32[2,16,8]{1,2,0:T(8,128)} %param.14) | copy-start | bytes 3076
  44.7 39.5 %collective-permute-start = (bf16[3,2,256,512]{3,2,1,0:T(8,128)(2,1)}, bf16[3,2,256,512]{3,2,1,0:T(8,128)(2,1)}, u32[]{:S(2)}, u32[]{:S(2)}) collective-permute-start(bf16[3,2,256,512]{3,2,1,0:T(8,128)(2,1)} %slice.20), channel_id=1, source_target_pairs={{0,4},{1,5},{2,6},{3,7},{4,8},{5,9},{6,10},{7,11},{8,12},{9,13},{1... | collective-permute-start | bytes 4718600 | tf_op jit(solution)/shard_map/ppermute | solution.py:25
  99.8 243.1 %all-to-all-start.2 = ((bf16[32,10,2,64,128]{4,3,2,1,0:T(8,128)(2,1)}), bf16[32,10,2,64,128]{4,3,2,1,0:T(8,128)(2,1)}, u32[]{:S(2)}, u32[]{:S(2)}) async-start(bf16[32,10,2,64,128]{4,3,2,1,0:T(8,128)(2,1)} %pick.1), calls=%async_computation.2 | async-start | bytes 20971520 | tf_op jit(solution)/shard_map/all_to_all | solution.py:232
  105.0 19.7 %copy-start.3 = (f32[16]{0:T(128)S(1)}, f32[16]{0:T(128)}, u32[]{:S(2)}) copy-start(f32[16]{0:T(128)} %param.15) | copy-start | bytes 196
  120.5 53.3 %collective-permute-start.1 = (bf16[256,512]{1,0:T(8,128)(2,1)S(1)}, bf16[256,512]{1,0:T(8,128)(2,1)S(1)}, u32[]{:S(2)}, u32[]{:S(2)}) collective-permute-start(bf16[256,512]{1,0:T(8,128)(2,1)S(1)} %get-tuple-element.12), channel_id=1, source_target_pairs={{0,1},{1,2},{2,3},{3,0},{4,5},{5,6},{6,7},{7,4},{8,9},{9,10},{10,1... | collective-permute-start | bytes 786440 | tf_op jit(solution)/shard_map/ppermute | solution.py:168
  121.7 52.1 %collective-permute-start.2 = (bf16[256,512]{1,0:T(8,128)(2,1)S(1)}, bf16[256,512]{1,0:T(8,128)(2,1)S(1)}, u32[]{:S(2)}, u32[]{:S(2)}) collective-permute-start(bf16[256,512]{1,0:T(8,128)(2,1)S(1)} %get-tuple-element.11), channel_id=1, source_target_pairs={{0,2},{1,3},{2,0},{3,1},{4,6},{5,7},{6,4},{7,5},{8,10},{9,11},{10,... | collective-permute-start | bytes 786440 | tf_op jit(solution)/shard_map/ppermute | solution.py:168
  122.9 59.7 %collective-permute-start.3 = (bf16[256,512]{1,0:T(8,128)(2,1)S(1)}, bf16[256,512]{1,0:T(8,128)(2,1)S(1)}, u32[]{:S(2)}, u32[]{:S(2)}) collective-permute-start(bf16[256,512]{1,0:T(8,128)(2,1)S(1)} %get-tuple-element.10), channel_id=1, source_target_pairs={{0,3},{1,0},{2,1},{3,2},{4,7},{5,4},{6,5},{7,6},{8,11},{9,8},{10,9... | collective-permute-start | bytes 786440 | tf_op jit(solution)/shard_map/ppermute | solution.py:168

commit v4 on v3

--- a/solution.py
+++ b/solution.py
@@ -79,18 +79,31 @@
     return lax.dot_general(query, key, (((1,), (1,)), ((), ())), preferred_element_type=jnp.float32)
 
 
-def band_kernel(q_ref, key_ref, value_ref, key_before, value_before, out_ref):
-    rows = q_ref.shape[2]
+def band_kernel(*refs):
+    own, before = refs[:GROUP], refs[GROUP : 2 * GROUP]
+    out_ref, query, key, value = refs[2 * GROUP :]
+    rows = query.shape[1]
     behind = BEHIND * rows
     place = lax.axis_index("blk")
     first = jnp.where(place < GROUP, behind, 0)
-    key = jnp.concatenate([key_before[...].reshape(behind, DH), key_ref[...].reshape(GROUP * rows, DH)], axis=0)
-    value = jnp.concatenate([value_before[...].reshape(behind, DH), value_ref[...].reshape(GROUP * rows, DH)], axis=0)
+    for shift in range(GROUP):
+        source = (place % GROUP - shift + GROUP) % GROUP
+        at = pl.multiple_of(behind + source * rows, rows)
+        query[source] = own[shift][0]
+        key[pl.ds(at, rows), :] = own[shift][1]
+        value[pl.ds(at, rows), :] = own[shift][2]
+
+        @pl.when(source >= GROUP - BEHIND)
+        def _():
+            earlier = pl.multiple_of((source - (GROUP - BEHIND)) * rows, rows)
+            key[pl.ds(earlier, rows), :] = before[shift][0]
+            value[pl.ds(earlier, rows), :] = before[shift][1]
+
     width = behind + QBLK
     for tile in range(GROUP * rows // QBLK):
         base = tile * QBLK
         member, start = divmod(base, rows)
-        scores = scores_of(q_ref[member, 0, start : start + QBLK, :], key[base : base + width, :])
+        scores = scores_of(query[member, start : start + QBLK, :], key[base : base + width, :])
         row = lax.broadcasted_iota(jnp.int32, scores.shape, 0)
         col = lax.broadcasted_iota(jnp.int32, scores.shape, 1)
         allowed = (col >= jnp.maximum(row, first - base)) & (col <= row + behind)
@@ -100,64 +113,70 @@
         out_ref[shift, start : start + QBLK, :] = result.astype(out_ref.dtype)
 
 
-def band(gathered, before):
-    members, _, rows, width = gathered.shape
-
-    def spec(which):
-        return pl.BlockSpec((members, 1, rows, DH), lambda h: (0, which, 0, h))
-
-    def spec_before(which):
-        return pl.BlockSpec((BEHIND, 1, rows, DH), lambda h: (0, which, 0, h))
-
+def band(own, before):
+    _, rows, width = own[0].shape
     return pl.pallas_call(
         band_kernel,
         grid=(width // DH,),
-        out_shape=jax.ShapeDtypeStruct((members, rows, width), jnp.bfloat16),
-        in_specs=[spec(0), spec(1), spec(2), spec_before(0), spec_before(1)],
-        out_specs=pl.BlockSpec((members, rows, DH), lambda h: (0, 0, h)),
+        out_shape=jax.ShapeDtypeStruct((GROUP, rows, width), jnp.bfloat16),
+        in_specs=[pl.BlockSpec((3, rows, DH), lambda h: (0, 0, h))] * GROUP
+        + [pl.BlockSpec((2, rows, DH), lambda h: (0, 0, h))] * GROUP,
+        out_specs=pl.BlockSpec((GROUP, rows, DH), lambda h: (0, 0, h)),
+        scratch_shapes=[
+            pltpu.VMEM((GROUP, rows, DH), jnp.bfloat16),
+            pltpu.VMEM(((GROUP + BEHIND) * rows, DH), jnp.bfloat16),
+            pltpu.VMEM(((GROUP + BEHIND) * rows, DH), jnp.bfloat16),
+        ],
         cost_estimate=pl.CostEstimate(
-            flops=2 * 2 * members * rows * 1024 * width,
-            bytes_accessed=members * rows * width * 14,
-            transcendentals=members * rows * 1024 * width // DH,
+            flops=2 * 2 * GROUP * rows * 1024 * width,
+            bytes_accessed=GROUP * rows * width * 14,
+            transcendentals=GROUP * rows * 1024 * width // DH,
         ),
         compiler_params=pltpu.CompilerParams(vmem_limit_bytes=56 << 20),
         name="band",
-    )(gathered, gathered, gathered, before, before)
-
-
-def pack_kernel(q_ref, k_ref, v_ref, out_ref):
+    )(*own, *before)
+
+
+def pack_kernel(member_ref, q_ref, k_ref, v_ref, out_ref):
     out_ref[0, 0] = q_ref[...]
     out_ref[0, 1] = k_ref[...]
     out_ref[0, 2] = v_ref[...]
 
 
-def pack(queries, keys, values):
+def pack(member, queries, keys, values):
     rows, width = queries.shape
     part = width // GROUP
-    spec = pl.BlockSpec((rows, part), lambda g: (0, g))
+    spec = pl.BlockSpec((rows, part), lambda s, m: (0, (m[0] + s) % GROUP))
     return pl.pallas_call(
         pack_kernel,
-        grid=(GROUP,),
+        grid_spec=pltpu.PrefetchScalarGridSpec(
+            num_scalar_prefetch=1,
+            grid=(GROUP,),
+            in_specs=[spec] * 3,
+            out_specs=pl.BlockSpec((1, 3, rows, part), lambda s, m: (s, 0, 0, 0)),
+        ),
         out_shape=jax.ShapeDtypeStruct((GROUP, 3, rows, part), queries.dtype),
-        in_specs=[spec] * 3,
-        out_specs=pl.BlockSpec((1, 3, rows, part), lambda g: (g, 0, 0, 0)),
         compiler_params=pltpu.CompilerParams(vmem_limit_bytes=56 << 20),
         name="pack",
-    )(queries, keys, values)
-
-
-def gather_heads(queries, keys, values):
+    )(member, queries, keys, values)
+
+
+def share_heads(packed):
     count = lax.axis_size("blk")
-    groups = [[g + i for i in range(GROUP)] for g in range(0, count, GROUP)]
-    gathered = lax.all_to_all(
-        pack(queries, keys, values),
-        "blk",
-        split_axis=0,
-        concat_axis=0,
-        axis_index_groups=groups,
-        tiled=True,
-    )
-    return gathered, from_behind(gathered[GROUP - BEHIND :, 1:], "blk", GROUP)
+
+    def target(i, shift):
+        return i // GROUP * GROUP + (i + shift) % GROUP
+
+    before = []
+    for shift in range(GROUP):
+        pairs = [
+            (i, target(i, shift) + GROUP) for i in range(count - GROUP) if i % GROUP >= GROUP - BEHIND
+        ]
+        before.append(lax.ppermute(packed[shift, 1:], "blk", pairs))
+    own = [packed[0]]
+    for shift in range(1, GROUP):
+        own.append(lax.ppermute(packed[shift], "blk", [(i, target(i, shift)) for i in range(count)]))
+    return own, before
 
 
 def return_rows(parts):
@@ -225,15 +244,17 @@
     peer_count = lax.axis_size("grp") * lax.axis_size("blk")
     capacity = max(2, 5 * target.shape[0] // (4 * peer_count))
     requests, arrival = plan_requests(target, slots.reshape(-1) * H + head_flat, peer_count, capacity)
+    member = (lax.axis_index("blk") % GROUP).astype(jnp.int32)[None]
+    packed = pack(member, queries, keys, values)
+    requests, packed = lax.optimization_barrier((requests, packed))
+    own, before = share_heads(packed)
     named = lax.all_to_all(requests, ("grp", "blk"), split_axis=0, concat_axis=0, tiled=True)
-    gathered, before = gather_heads(queries, keys, values)
-    named, before = lax.optimization_barrier((named, before))
     picked = pick(named.reshape(-1), memory_keys, memory_values, peer_count)
+    picked, own, before = lax.optimization_barrier((picked, own, before))
     arrived = lax.all_to_all(picked, ("grp", "blk"), split_axis=0, concat_axis=0, tiled=True)
     arrived = arrived.reshape(peer_count * capacity, 2, MB, DH)
-    band_out = return_rows(band(gathered, before))
-    member = lax.axis_index("blk") % GROUP
-    arrival = jnp.concatenate([arrival, member[None].astype(jnp.int32)])
+    band_out = return_rows(band(own, before))
+    arrival = jnp.concatenate([arrival, member])
     return memory(arrival, jax.nn.sigmoid(gate_logit), queries, band_out, arrived)
 
 

time: 366 us -> 368 us (level)
  blocking collectives: 74.6 us -> 41.8 us
  waiting for transfers between devices: 217 us -> 235 us
  Pallas kernels: 52.1 us -> 59.2 us
  starting transfers between devices: 12 us -> 18.1 us
    all_to_all x1 -> x0, blocking collectives: 39.2 us -> none  [gather_heads(): lax.all_to_all(pack(queries, keys, values), 'blk', split_axis=0, concat_a...]
    ppermute x1 -> x7, waiting for transfers between devices: 0.01 us -> 16.7 us  [the longest x4 16.7 us: share_heads(): before.append(lax.ppermute(packed[shift, 1:], 'blk', pairs))]
    ppermute x1 -> x7, starting transfers between devices: 3.19 us -> 11.6 us  [the longest x3 7.05 us: share_heads(): lax.ppermute(packed[shift], 'blk', [(i, target(i, shift)) for i in range(...]
    pallas_call x1, Pallas kernels: 14.9 us -> 21.4 us  [pick(): pl.pallas_call(functools.partial(pick_kernel, peers=peers, each=each), ou...]
    all_to_all x1, blocking collectives: 35.4 us -> 41.8 us  [local(): lax.all_to_all(requests, ('grp', 'blk'), split_axis=0, concat_axis=0, til...]
  transfers between devices with their start and end apart: 5 -> 11, of which waited for: 3 -> 4; matrix products, arithmetic and copies ran while one was open for 1% -> 2% of each run, Pallas kernels for 4% -> 10%
where the time goes in v4:
time: 368 us; the launch traced here: 365 us
  waiting for transfers between devices  235 us (64%)
  Pallas kernels  59.2 us (16%)
  blocking collectives  41.8 us (11%)
  starting transfers between devices  18.1 us (5%)
  local copies, waits for them, and re-layouts  6.48 us (2%)
  other arithmetic  3.98 us (1%)
    all_to_all x1, waiting for transfers between devices, local(): lax.all_to_all(picked, ('grp', 'blk'), split_axis=0, concat_axis=0, tiled...  162 us
    ppermute x3, waiting for transfers between devices, return_rows(): back.append(lax.ppermute(parts[shift], 'blk', pairs))  56.6 us
    all_to_all x1, blocking collectives, local(): lax.all_to_all(requests, ('grp', 'blk'), split_axis=0, concat_axis=0, til...  41.8 us
    pallas_call x1, Pallas kernels, pick(): pl.pallas_call(functools.partial(pick_kernel, peers=peers, each=each), ou...  21.4 us
    pallas_call x1, Pallas kernels, memory(): pl.pallas_call(memory_kernel, grid_spec=pltpu.PrefetchScalarGridSpec(num_...  18.8 us
    ppermute x4, waiting for transfers between devices, share_heads(): before.append(lax.ppermute(packed[shift, 1:], 'blk', pairs))  16.7 us
    pallas_call x1, Pallas kernels, band(): pl.pallas_call(band_kernel, grid=(width // DH,), out_shape=jax.ShapeDtype...  14.8 us
  transfers between devices with their start and end apart: 11, of which 4 were waited for; matrix products, arithmetic and copies ran while one was open for 2% of the time, Pallas kernels for 10%

profile of v4, /device:TPU:17, one launch (start us, length us, event | category | flops | bytes accessed | tf_op | source)
XLA Modules:
  0.0 364.9 jit_solution(17634214280144511515)
XLA Ops:
  0.0 0.8 copy.14
  1.1 0.7 iota_add_fusion
  2.2 4.2 %pack.1 = bf16[4,3,256,512]{3,2,1,0:T(8,128)(2,1)} custom-call(s32[1]{0:T(128)} %bitcast.member_ref, bf16[256,2048]{1,0:T(8,128)(2,1)} %q_ref.3, bf16[256,2048]{1,0:T(8,128)(2,1)} %k_ref.1, bf16[256,2048]{1,0:T(8,128)(2,1)} %v_ref.1), custom_call_target="tpu_custom_call" | custom-call | tf_op jit(solution)/shard_map/pack/pallas_call | solution.py:150
  6.4 1.8 slice_bitcast_fusion.4
  8.9 1.3 collective-permute-start.4
  10.2 1.1 slice_bitcast_fusion
  11.3 4.7 %collective-permute-start = (bf16[3,256,512]{2,1,0:T(8,128)(2,1)S(1)}, bf16[3,256,512]{2,1,0:T(8,128)(2,1)}, u32[]{:S(2)}, u32[]{:S(2)}) collective-permute-start(bf16[3,256,512]{2,1,0:T(8,128)(2,1)S(1)} %get-tuple-element.33), channel_id=1, source_target_pairs={{0,1},{1,2},{2,3},{3,0},{4,5},{5,6},{6,7},{7,4},{8,9},{9,10},{10,1... | collective-permute-start | bytes 2359304 | tf_op jit(solution)/shard_map/ppermute | solution.py:178
  16.0 0.9 collective-permute-start.1
  16.9 1.5 collective-permute-start.2
  18.3 1.3 collective-permute-start.5
  19.6 16.7 %collective-permute-done.4.refs_5_ = bf16[2,256,512]{2,1,0:T(8,128)(2,1)S(1)} collective-permute-done((bf16[2,256,512]{2,1,0:T(8,128)(2,1)S(1)}, bf16[2,256,512]{2,1,0:T(8,128)(2,1)S(1)}, u32[]{:S(2)}, u32[]{:S(2)}) %collective-permute-start.4) | collective-permute-done | bytes 524320 | tf_op jit(solution)/shard_map/ppermute | solution.py:175
  36.3 1.3 collective-permute-start.6
  37.7 41.8 %all_to_all.14 = s32[32,1,10]{2,1,0:T(1,128)S(1)} all-to-all(s32[32,1,10]{2,1,0:T(1,128)S(1)} %bitcast.33), channel_id=1, replica_groups=mesh['grp'=2,'blk'=16] {'grp','blk'}, dimensions={0} | all-to-all | bytes 2560 | tf_op jit(solution)/shard_map/all_to_all | solution.py:251
  81.3 21.4 %pick.1 = bf16[32,10,2,64,128]{4,3,2,1,0:T(8,128)(2,1)} custom-call(s32[320]{0:T(512)} %reshape.42.req_ref, bf16[8,64,2048]{2,1,0:T(8,128)(2,1)} %key_ref.1, bf16[8,64,2048]{2,1,0:T(8,128)(2,1)} %value_ref.1), custom_call_target="tpu_custom_call" | custom-call | tf_op jit(solution)/shard_map/pick/pallas_call | solution.py:51
  102.8 3.5 all-to-all-start.1
  106.3 14.8 %band.1 = bf16[4,256,512]{2,1,0:T(8,128)(2,1)} custom-call(bf16[3,256,512]{2,1,0:T(8,128)(2,1)} %get-tuple-element.18.refs_0_, bf16[3,256,512]{2,1,0:T(8,128)(2,1)} %collective-permute-done.refs_1_, bf16[3,256,512]{2,1,0:T(8,128)(2,1)} %collective-permute-done.1.refs_2_, bf16[3,256,512]{2,1,0:T(8,128)(2,1)} %collective-permute-done.2.refs_3_, ...), custom_call_target="tpu_custom_call" | custom-call | flops 2147483648 | bytes 7340032 | tf_op jit(solution)/shard_map/band/pallas_call | solution.py:118
  121.1 1.3 fusion.1
  123.0 1.2 collective-permute-start.8
  124.2 1.2 collective-permute-start.9
  126.5 48.7 %collective-permute-done.7 = bf16[256,512]{1,0:T(8,128)(2,1)S(1)} collective-permute-done((bf16[256,512]{1,0:T(8,128)(2,1)S(1)}, bf16[256,512]{1,0:T(8,128)(2,1)S(1)}, u32[]{:S(2)}, u32[]{:S(2)}) %collective-permute-start.7) | collective-permute-done | bytes 262176 | tf_op jit(solution)/shard_map/ppermute | solution.py:187
  175.2 7.9 %collective-permute-done.9 = bf16[256,512]{1,0:T(8,128)(2,1)S(1)} collective-permute-done((bf16[256,512]{1,0:T(8,128)(2,1)S(1)}, bf16[256,512]{1,0:T(8,128)(2,1)S(1)}, u32[]{:S(2)}, u32[]{:S(2)}) %collective-permute-start.9) | collective-permute-done | bytes 262176 | tf_op jit(solution)/shard_map/ppermute | solution.py:187
  183.1 1.1 pad_maximum_fusion.band_ref
  184.2 161.9 %all-to-all-done.1 = bf16[32,10,2,64,128]{4,3,2,1,0:T(8,128)(2,1)} async-done(((bf16[32,10,2,64,128]{4,3,2,1,0:T(8,128)(2,1)}), bf16[32,10,2,64,128]{4,3,2,1,0:T(8,128)(2,1)}, u32[]{:S(2)}, u32[]{:S(2)}) %all-to-all-start.1) | async-done | bytes 10485792 | tf_op jit(solution)/shard_map/all_to_all | solution.py:254
  346.1 18.8 %memory.1 = bf16[256,2048]{1,0:T(8,128)(2,1)} custom-call(s32[257]{0:T(512)} %pad_add_fusion.arrival_ref, f32[16]{0:T(128)} %add_divide_fusion.gate_ref, bf16[256,2048]{1,0:T(8,128)(2,1)} %q_ref.3, bf16[4,256,512]{2,1,0:T(8,128)(2,1)} %pad_maximum_fusion.band_ref, ...), custom_call_target="tpu_custom_call" | custom-call | tf_op jit(solution)/shard_map/memory/pallas_call | solution.py:216
  (29 shorter events, 5.1 us)
Async XLA Ops:
  6.4 3.8 %copy-start = (bf16[4,3,256,512]{3,2,1,0:T(8,128)(2,1)S(1)}, bf16[4,3,256,512]{3,2,1,0:T(8,128)(2,1)}, u32[]{:S(2)}) copy-start(bf16[4,3,256,512]{3,2,1,0:T(8,128)(2,1)} %pack.1) | copy-start | bytes 9437188
  8.2 10.2 %collective-permute-start.3 = (bf16[2,256,512]{2,1,0:T(8,128)(2,1)S(1)}, bf16[2,256,512]{2,1,0:T(8,128)(2,1)S(1)}, u32[]{:S(2)}, u32[]{:S(2)}) collective-permute-start(bf16[2,256,512]{2,1,0:T(8,128)(2,1)S(1)} %get-tuple-element.30), channel_id=1, source_target_pairs={{1,5},{2,6},{3,7},{5,9},{6,10},{7,11},{9,13},{10,14},{11,15},{17,2... | collective-permute-start | bytes 1572872 | tf_op jit(solution)/shard_map/ppermute | solution.py:175
  8.9 27.4 %collective-permute-start.4 = (bf16[2,256,512]{2,1,0:T(8,128)(2,1)S(1)}, bf16[2,256,512]{2,1,0:T(8,128)(2,1)S(1)}, u32[]{:S(2)}, u32[]{:S(2)}) collective-permute-start(bf16[2,256,512]{2,1,0:T(8,128)(2,1)S(1)} %get-tuple-element.29), channel_id=1, source_target_pairs={{1,6},{2,7},{3,4},{5,10},{6,11},{7,8},{9,14},{10,15},{11,12},{17,2... | collective-permute-start | bytes 1572872 | tf_op jit(solution)/shard_map/ppermute | solution.py:175
  11.3 91.4 %collective-permute-start = (bf16[3,256,512]{2,1,0:T(8,128)(2,1)S(1)}, bf16[3,256,512]{2,1,0:T(8,128)(2,1)}, u32[]{:S(2)}, u32[]{:S(2)}) collective-permute-start(bf16[3,256,512]{2,1,0:T(8,128)(2,1)S(1)} %get-tuple-element.33), channel_id=1, source_target_pairs={{0,1},{1,2},{2,3},{3,0},{4,5},{5,6},{6,7},{7,4},{8,9},{9,10},{10,1... | collective-permute-start | bytes 2359304 | tf_op jit(solution)/shard_map/ppermute | solution.py:178
  16.0 86.8 %collective-permute-start.1 = (bf16[3,256,512]{2,1,0:T(8,128)(2,1)S(1)}, bf16[3,256,512]{2,1,0:T(8,128)(2,1)}, u32[]{:S(2)}, u32[]{:S(2)}) collective-permute-start(bf16[3,256,512]{2,1,0:T(8,128)(2,1)S(1)} %get-tuple-element.32), channel_id=1, source_target_pairs={{0,2},{1,3},{2,0},{3,1},{4,6},{5,7},{6,4},{7,5},{8,10},{9,11},{10,... | collective-permute-start | bytes 2359304 | tf_op jit(solution)/shard_map/ppermute | solution.py:178
  16.9 85.9 %collective-permute-start.2 = (bf16[3,256,512]{2,1,0:T(8,128)(2,1)S(1)}, bf16[3,256,512]{2,1,0:T(8,128)(2,1)}, u32[]{:S(2)}, u32[]{:S(2)}) collective-permute-start(bf16[3,256,512]{2,1,0:T(8,128)(2,1)S(1)} %get-tuple-element.31), channel_id=1, source_target_pairs={{0,3},{1,0},{2,1},{3,2},{4,7},{5,4},{6,5},{7,6},{8,11},{9,8},{10,9... | collective-permute-start | bytes 2359304 | tf_op jit(solution)/shard_map/ppermute | solution.py:178
  18.3 19.3 %copy-start.1 = (bf16[2,256,512]{2,1,0:T(8,128)(2,1)}, bf16[2,256,512]{2,1,0:T(8,128)(2,1)S(1)}, u32[]{:S(2)}) copy-start(bf16[2,256,512]{2,1,0:T(8,128)(2,1)S(1)} %collective-permute-done.3.refs_4_) | copy-start | bytes 1572868
  18.3 84.4 %collective-permute-start.5 = (bf16[2,256,512]{2,1,0:T(8,128)(2,1)S(1)}, bf16[2,256,512]{2,1,0:T(8,128)(2,1)}, u32[]{:S(2)}, u32[]{:S(2)}) collective-permute-start(bf16[2,256,512]{2,1,0:T(8,128)(2,1)S(1)} %get-tuple-element.28), channel_id=1, source_target_pairs={{1,7},{2,4},{3,5},{5,11},{6,8},{7,9},{9,15},{10,12},{11,13},{17,23... | collective-permute-start | bytes 1572872 | tf_op jit(solution)/shard_map/ppermute | solution.py:175
  36.3 1.3 copy-start.2
  36.3 66.4 %collective-permute-start.6 = (bf16[2,256,512]{2,1,0:T(8,128)(2,1)S(1)}, bf16[2,256,512]{2,1,0:T(8,128)(2,1)}, u32[]{:S(2)}, u32[]{:S(2)}) collective-permute-start(bf16[2,256,512]{2,1,0:T(8,128)(2,1)S(1)} %get-tuple-element.27), channel_id=1, source_target_pairs={{1,4},{2,5},{3,6},{5,8},{6,9},{7,10},{9,12},{10,13},{11,14},{17,20... | collective-permute-start | bytes 1572872 | tf_op jit(solution)/shard_map/ppermute | solution.py:175
  102.8 243.3 %all-to-all-start.1 = ((bf16[32,10,2,64,128]{4,3,2,1,0:T(8,128)(2,1)}), bf16[32,10,2,64,128]{4,3,2,1,0:T(8,128)(2,1)}, u32[]{:S(2)}, u32[]{:S(2)}) async-start(bf16[32,10,2,64,128]{4,3,2,1,0:T(8,128)(2,1)} %pick.1), calls=%async_computation.1 | async-start | bytes 20971520 | tf_op jit(solution)/shard_map/all_to_all | solution.py:254
  106.3 19.7 %copy-start.3 = (f32[16]{0:T(128)S(1)}, f32[16]{0:T(128)}, u32[]{:S(2)}) copy-start(f32[16]{0:T(128)} %param.15) | copy-start | bytes 196
  122.4 52.8 %collective-permute-start.7 = (bf16[256,512]{1,0:T(8,128)(2,1)S(1)}, bf16[256,512]{1,0:T(8,128)(2,1)S(1)}, u32[]{:S(2)}, u32[]{:S(2)}) collective-permute-start(bf16[256,512]{1,0:T(8,128)(2,1)S(1)} %get-tuple-element.38), channel_id=1, source_target_pairs={{0,1},{1,2},{2,3},{3,0},{4,5},{5,6},{6,7},{7,4},{8,9},{9,10},{10,1... | collective-permute-start | bytes 786440 | tf_op jit(solution)/shard_map/ppermute | solution.py:187
  123.0 52.2 %collective-permute-start.8 = (bf16[256,512]{1,0:T(8,128)(2,1)S(1)}, bf16[256,512]{1,0:T(8,128)(2,1)S(1)}, u32[]{:S(2)}, u32[]{:S(2)}) collective-permute-start(bf16[256,512]{1,0:T(8,128)(2,1)S(1)} %get-tuple-element.37), channel_id=1, source_target_pairs={{0,2},{1,3},{2,0},{3,1},{4,6},{5,7},{6,4},{7,5},{8,10},{9,11},{10,... | collective-permute-start | bytes 786440 | tf_op jit(solution)/shard_map/ppermute | solution.py:187
  124.2 58.9 %collective-permute-start.9 = (bf16[256,512]{1,0:T(8,128)(2,1)S(1)}, bf16[256,512]{1,0:T(8,128)(2,1)S(1)}, u32[]{:S(2)}, u32[]{:S(2)}) collective-permute-start(bf16[256,512]{1,0:T(8,128)(2,1)S(1)} %get-tuple-element.36), channel_id=1, source_target_pairs={{0,3},{1,0},{2,1},{3,2},{4,7},{5,4},{6,5},{7,6},{8,11},{9,8},{10,9... | collective-permute-start | bytes 786440 | tf_op jit(solution)/shard_map/ppermute | solution.py:187

commit v5 on v4

--- a/solution.py
+++ b/solution.py
@@ -246,11 +246,10 @@
     requests, arrival = plan_requests(target, slots.reshape(-1) * H + head_flat, peer_count, capacity)
     member = (lax.axis_index("blk") % GROUP).astype(jnp.int32)[None]
     packed = pack(member, queries, keys, values)
-    requests, packed = lax.optimization_barrier((requests, packed))
+    named = lax.all_to_all(requests, ("grp", "blk"), split_axis=0, concat_axis=0, tiled=True)
+    named, packed = lax.optimization_barrier((named, packed))
     own, before = share_heads(packed)
-    named = lax.all_to_all(requests, ("grp", "blk"), split_axis=0, concat_axis=0, tiled=True)
     picked = pick(named.reshape(-1), memory_keys, memory_values, peer_count)
-    picked, own, before = lax.optimization_barrier((picked, own, before))
     arrived = lax.all_to_all(picked, ("grp", "blk"), split_axis=0, concat_axis=0, tiled=True)
     arrived = arrived.reshape(peer_count * capacity, 2, MB, DH)
     band_out = return_rows(band(own, before))

time: 368 us -> 374 us (1.016)
  blocking collectives: 41.8 us -> 0 us
  waiting for transfers between devices: 235 us -> 275 us
  starting transfers between devices: 18.1 us -> 40.6 us
  Pallas kernels: 59.2 us -> 46.5 us
    ppermute x4, waiting for transfers between devices: 16.7 us -> 265 us  [share_heads(): before.append(lax.ppermute(packed[shift, 1:], 'blk', pairs))]
    all_to_all x1, waiting for transfers between devices: 162 us -> 0.01 us  [local(): lax.all_to_all(picked, ('grp', 'blk'), split_axis=0, concat_axis=0, tiled...]
    ppermute x3, waiting for transfers between devices: 56.6 us -> 9.29 us  [return_rows(): back.append(lax.ppermute(parts[shift], 'blk', pairs))]
    all_to_all x1 -> x0, blocking collectives: 41.8 us -> none  [local(): lax.all_to_all(requests, ('grp', 'blk'), split_axis=0, concat_axis=0, til...]
    pallas_call x1, Pallas kernels: 21.4 us -> 8.65 us  [pick(): pl.pallas_call(functools.partial(pick_kernel, peers=peers, each=each), ou...]
    all_to_all x1, starting transfers between devices: 3.49 us -> 15.9 us  [local(): lax.all_to_all(picked, ('grp', 'blk'), split_axis=0, concat_axis=0, tiled...]
    all_to_all x0 -> x1, starting transfers between devices: none -> 6.25 us  [local(): lax.all_to_all(requests, ('grp', 'blk'), split_axis=0, concat_axis=0, til...]
    ppermute x3, starting transfers between devices: 2.97 us -> 6.97 us  [return_rows(): back.append(lax.ppermute(parts[shift], 'blk', pairs))]
  transfers between devices with their start and end apart: 11 -> 12, of which waited for: 4 -> 7; matrix products, arithmetic and copies ran while one was open for 2% -> 1% of each run, Pallas kernels for 10% -> 5%
where the time goes in v5:
time: 374 us; the launch traced here: 371 us
  waiting for transfers between devices  275 us (74%)
  Pallas kernels  46.5 us (12%)
  starting transfers between devices  40.6 us (11%)
  local copies, waits for them, and re-layouts  6.47 us (2%)
    ppermute x4, waiting for transfers between devices, share_heads(): before.append(lax.ppermute(packed[shift, 1:], 'blk', pairs))  265 us
    pallas_call x1, Pallas kernels, memory(): pl.pallas_call(memory_kernel, grid_spec=pltpu.PrefetchScalarGridSpec(num_...  18.8 us
    all_to_all x1, starting transfers between devices, local(): lax.all_to_all(picked, ('grp', 'blk'), split_axis=0, concat_axis=0, tiled...  15.9 us
    pallas_call x1, Pallas kernels, band(): pl.pallas_call(band_kernel, grid=(width // DH,), out_shape=jax.ShapeDtype...  14.8 us
    ppermute x3, waiting for transfers between devices, return_rows(): back.append(lax.ppermute(parts[shift], 'blk', pairs))  9.29 us
    pallas_call x1, Pallas kernels, pick(): pl.pallas_call(functools.partial(pick_kernel, peers=peers, each=each), ou...  8.65 us
  transfers between devices with their start and end apart: 12, of which 7 were waited for; matrix products, arithmetic and copies ran while one was open for 1% of the time, Pallas kernels for 5%

profile of v5, /device:TPU:17, one launch (start us, length us, event | category | flops | bytes accessed | tf_op | source)
XLA Modules:
  0.0 371.5 jit_solution(15603051888633833978)
XLA Ops:
  0.0 0.8 copy.14
  2.8 6.2 %all-to-all-start = ((s32[32,1,10]{2,1,0:T(1,128)}), s32[32,1,10]{2,1,0:T(1,128)S(1)}, u32[]{:S(2)}, u32[]{:S(2)}) async-start(s32[32,1,10]{2,1,0:T(1,128)} %bitcast.1), calls=%async_computation | async-start | bytes 32768 | tf_op jit(solution)/shard_map/all_to_all | solution.py:249
  9.1 4.2 %pack.1 = bf16[4,3,256,512]{3,2,1,0:T(8,128)(2,1)} custom-call(s32[1]{0:T(128)} %bitcast.member_ref, bf16[256,2048]{1,0:T(8,128)(2,1)} %q_ref.3, bf16[256,2048]{1,0:T(8,128)(2,1)} %k_ref.1, bf16[256,2048]{1,0:T(8,128)(2,1)} %v_ref.1), custom_call_target="tpu_custom_call" | custom-call | tf_op jit(solution)/shard_map/pack/pallas_call | solution.py:150
  14.3 8.7 %pick.1 = bf16[32,10,2,64,128]{4,3,2,1,0:T(8,128)(2,1)} custom-call(s32[320]{0:T(512)} %reshape.39.req_ref, bf16[8,64,2048]{2,1,0:T(8,128)(2,1)} %key_ref.1, bf16[8,64,2048]{2,1,0:T(8,128)(2,1)} %value_ref.1), custom_call_target="tpu_custom_call" | custom-call | tf_op jit(solution)/shard_map/pick/pallas_call | solution.py:51
  23.0 15.9 %all-to-all-start.1 = ((bf16[32,10,2,64,128]{4,3,2,1,0:T(8,128)(2,1)}), bf16[32,10,2,64,128]{4,3,2,1,0:T(8,128)(2,1)}, u32[]{:S(2)}, u32[]{:S(2)}) async-start(bf16[32,10,2,64,128]{4,3,2,1,0:T(8,128)(2,1)} %pick.1), calls=%async_computation.1 | async-start | bytes 20971520 | tf_op jit(solution)/shard_map/all_to_all | solution.py:253
  39.8 1.3 collective-permute-start.4
  41.1 1.1 slice_bitcast_fusion
  42.2 4.6 %collective-permute-start = (bf16[3,256,512]{2,1,0:T(8,128)(2,1)S(1)}, bf16[3,256,512]{2,1,0:T(8,128)(2,1)S(1)}, u32[]{:S(2)}, u32[]{:S(2)}) collective-permute-start(bf16[3,256,512]{2,1,0:T(8,128)(2,1)S(1)} %get-tuple-element.15), channel_id=1, source_target_pairs={{0,1},{1,2},{2,3},{3,0},{4,5},{5,6},{6,7},{7,4},{8,9},{9,10},{10,1... | collective-permute-start | bytes 2359304 | tf_op jit(solution)/shard_map/ppermute | solution.py:178
  46.7 0.9 collective-permute-start.1
  47.6 1.5 collective-permute-start.2
  49.1 1.3 collective-permute-start.5
  50.4 249.2 %collective-permute-done.4.refs_5_ = bf16[2,256,512]{2,1,0:T(8,128)(2,1)S(1)} collective-permute-done((bf16[2,256,512]{2,1,0:T(8,128)(2,1)S(1)}, bf16[2,256,512]{2,1,0:T(8,128)(2,1)S(1)}, u32[]{:S(2)}, u32[]{:S(2)}) %collective-permute-start.4) | collective-permute-done | bytes 524320 | tf_op jit(solution)/shard_map/ppermute | solution.py:175
  299.6 1.3 collective-permute-start.6
  300.9 6.6 %collective-permute-done.5.refs_6_ = bf16[2,256,512]{2,1,0:T(8,128)(2,1)S(1)} collective-permute-done((bf16[2,256,512]{2,1,0:T(8,128)(2,1)S(1)}, bf16[2,256,512]{2,1,0:T(8,128)(2,1)S(1)}, u32[]{:S(2)}, u32[]{:S(2)}) %collective-permute-start.5) | collective-permute-done | bytes 524320 | tf_op jit(solution)/shard_map/ppermute | solution.py:175
  307.4 9.1 %collective-permute-done.6.refs_7_ = bf16[2,256,512]{2,1,0:T(8,128)(2,1)S(1)} collective-permute-done((bf16[2,256,512]{2,1,0:T(8,128)(2,1)S(1)}, bf16[2,256,512]{2,1,0:T(8,128)(2,1)S(1)}, u32[]{:S(2)}, u32[]{:S(2)}) %collective-permute-start.6) | collective-permute-done | bytes 524320 | tf_op jit(solution)/shard_map/ppermute | solution.py:175
  318.1 14.8 %band.1 = bf16[4,256,512]{2,1,0:T(8,128)(2,1)} custom-call(bf16[3,256,512]{2,1,0:T(8,128)(2,1)} %get-tuple-element.16.refs_0_, bf16[3,256,512]{2,1,0:T(8,128)(2,1)} %copy-done.1, bf16[3,256,512]{2,1,0:T(8,128)(2,1)} %copy-done.2, bf16[3,256,512]{2,1,0:T(8,128)(2,1)} %copy-done.3, bf16[2,256,512]{2,1,0:T(8,128)(2,1)} %copy-done.4, ...), custom_call_target="tpu_custom_call" | custom-call | flops 2147483648 | bytes 7340032 | tf_op jit(solution)/shard_map/band/pallas_call | solution.py:118
  332.9 1.3 fusion.1
  334.2 4.4 %collective-permute-start.7 = (bf16[256,512]{1,0:T(8,128)(2,1)S(1)}, bf16[256,512]{1,0:T(8,128)(2,1)S(1)}, u32[]{:S(2)}, u32[]{:S(2)}) collective-permute-start(bf16[256,512]{1,0:T(8,128)(2,1)S(1)} %get-tuple-element.20), channel_id=1, source_target_pairs={{0,1},{1,2},{2,3},{3,0},{4,5},{5,6},{6,7},{7,4},{8,9},{9,10},{10,1... | collective-permute-start | bytes 786440 | tf_op jit(solution)/shard_map/ppermute | solution.py:187
  338.9 2.3 collective-permute-start.9
  342.3 1.4 collective-permute-done.7
  343.7 6.0 %collective-permute-done.8 = bf16[256,512]{1,0:T(8,128)(2,1)S(1)} collective-permute-done((bf16[256,512]{1,0:T(8,128)(2,1)S(1)}, bf16[256,512]{1,0:T(8,128)(2,1)S(1)}, u32[]{:S(2)}, u32[]{:S(2)}) %collective-permute-start.8) | collective-permute-done | bytes 262176 | tf_op jit(solution)/shard_map/ppermute | solution.py:187
  349.7 1.9 collective-permute-done.9
  351.6 1.1 pad_maximum_fusion.band_ref
  352.7 18.8 %memory.1 = bf16[256,2048]{1,0:T(8,128)(2,1)} custom-call(s32[257]{0:T(512)} %pad_add_fusion.arrival_ref, f32[16]{0:T(128)} %add_divide_fusion.gate_ref, bf16[256,2048]{1,0:T(8,128)(2,1)} %q_ref.3, bf16[4,256,512]{2,1,0:T(8,128)(2,1)} %pad_maximum_fusion.band_ref, ...), custom_call_target="tpu_custom_call" | custom-call | tf_op jit(solution)/shard_map/memory/pallas_call | solution.py:216
  (38 shorter events, 6.9 us)
Async XLA Ops:
  2.8 10.9 %all-to-all-start = ((s32[32,1,10]{2,1,0:T(1,128)}), s32[32,1,10]{2,1,0:T(1,128)S(1)}, u32[]{:S(2)}, u32[]{:S(2)}) async-start(s32[32,1,10]{2,1,0:T(1,128)} %bitcast.1), calls=%async_computation | async-start | bytes 32768 | tf_op jit(solution)/shard_map/all_to_all | solution.py:249
  23.0 15.9 %copy-start = (bf16[4,3,256,512]{3,2,1,0:T(8,128)(2,1)S(1)}, bf16[4,3,256,512]{3,2,1,0:T(8,128)(2,1)}, u32[]{:S(2)}) copy-start(bf16[4,3,256,512]{3,2,1,0:T(8,128)(2,1)} %pack.1) | copy-start | bytes 9437188
  23.0 329.7 %all-to-all-start.1 = ((bf16[32,10,2,64,128]{4,3,2,1,0:T(8,128)(2,1)}), bf16[32,10,2,64,128]{4,3,2,1,0:T(8,128)(2,1)}, u32[]{:S(2)}, u32[]{:S(2)}) async-start(bf16[32,10,2,64,128]{4,3,2,1,0:T(8,128)(2,1)} %pick.1), calls=%async_computation.1 | async-start | bytes 20971520 | tf_op jit(solution)/shard_map/all_to_all | solution.py:253
  39.1 10.0 %collective-permute-start.3 = (bf16[2,256,512]{2,1,0:T(8,128)(2,1)S(1)}, bf16[2,256,512]{2,1,0:T(8,128)(2,1)S(1)}, u32[]{:S(2)}, u32[]{:S(2)}) collective-permute-start(bf16[2,256,512]{2,1,0:T(8,128)(2,1)S(1)} %get-tuple-element.12), channel_id=1, source_target_pairs={{1,5},{2,6},{3,7},{5,9},{6,10},{7,11},{9,13},{10,14},{11,15},{17,2... | collective-permute-start | bytes 1572872 | tf_op jit(solution)/shard_map/ppermute | solution.py:175
  39.8 259.8 %collective-permute-start.4 = (bf16[2,256,512]{2,1,0:T(8,128)(2,1)S(1)}, bf16[2,256,512]{2,1,0:T(8,128)(2,1)S(1)}, u32[]{:S(2)}, u32[]{:S(2)}) collective-permute-start(bf16[2,256,512]{2,1,0:T(8,128)(2,1)S(1)} %get-tuple-element.11), channel_id=1, source_target_pairs={{1,6},{2,7},{3,4},{5,10},{6,11},{7,8},{9,14},{10,15},{11,12},{17,2... | collective-permute-start | bytes 1572872 | tf_op jit(solution)/shard_map/ppermute | solution.py:175
  42.2 274.3 %collective-permute-start = (bf16[3,256,512]{2,1,0:T(8,128)(2,1)S(1)}, bf16[3,256,512]{2,1,0:T(8,128)(2,1)S(1)}, u32[]{:S(2)}, u32[]{:S(2)}) collective-permute-start(bf16[3,256,512]{2,1,0:T(8,128)(2,1)S(1)} %get-tuple-element.15), channel_id=1, source_target_pairs={{0,1},{1,2},{2,3},{3,0},{4,5},{5,6},{6,7},{7,4},{8,9},{9,10},{10,1... | collective-permute-start | bytes 2359304 | tf_op jit(solution)/shard_map/ppermute | solution.py:178
  46.7 269.8 %collective-permute-start.1 = (bf16[3,256,512]{2,1,0:T(8,128)(2,1)S(1)}, bf16[3,256,512]{2,1,0:T(8,128)(2,1)S(1)}, u32[]{:S(2)}, u32[]{:S(2)}) collective-permute-start(bf16[3,256,512]{2,1,0:T(8,128)(2,1)S(1)} %get-tuple-element.14), channel_id=1, source_target_pairs={{0,2},{1,3},{2,0},{3,1},{4,6},{5,7},{6,4},{7,5},{8,10},{9,11},{10,... | collective-permute-start | bytes 2359304 | tf_op jit(solution)/shard_map/ppermute | solution.py:178
  47.6 268.9 %collective-permute-start.2 = (bf16[3,256,512]{2,1,0:T(8,128)(2,1)S(1)}, bf16[3,256,512]{2,1,0:T(8,128)(2,1)S(1)}, u32[]{:S(2)}, u32[]{:S(2)}) collective-permute-start(bf16[3,256,512]{2,1,0:T(8,128)(2,1)S(1)} %get-tuple-element.13), channel_id=1, source_target_pairs={{0,3},{1,0},{2,1},{3,2},{4,7},{5,4},{6,5},{7,6},{8,11},{9,8},{10,9... | collective-permute-start | bytes 2359304 | tf_op jit(solution)/shard_map/ppermute | solution.py:178
  49.1 267.4 %copy-start.4 = (bf16[2,256,512]{2,1,0:T(8,128)(2,1)}, bf16[2,256,512]{2,1,0:T(8,128)(2,1)S(1)}, u32[]{:S(2)}) copy-start(bf16[2,256,512]{2,1,0:T(8,128)(2,1)S(1)} %collective-permute-done.3.refs_4_) | copy-start | bytes 1572868
  49.1 258.3 %collective-permute-start.5 = (bf16[2,256,512]{2,1,0:T(8,128)(2,1)S(1)}, bf16[2,256,512]{2,1,0:T(8,128)(2,1)S(1)}, u32[]{:S(2)}, u32[]{:S(2)}) collective-permute-start(bf16[2,256,512]{2,1,0:T(8,128)(2,1)S(1)} %get-tuple-element.10), channel_id=1, source_target_pairs={{1,7},{2,4},{3,5},{5,11},{6,8},{7,9},{9,15},{10,12},{11,13},{17,23... | collective-permute-start | bytes 1572872 | tf_op jit(solution)/shard_map/ppermute | solution.py:175
  299.6 17.0 %copy-start.5 = (bf16[2,256,512]{2,1,0:T(8,128)(2,1)}, bf16[2,256,512]{2,1,0:T(8,128)(2,1)S(1)}, u32[]{:S(2)}) copy-start(bf16[2,256,512]{2,1,0:T(8,128)(2,1)S(1)} %collective-permute-done.4.refs_5_) | copy-start | bytes 1572868
  299.6 16.9 %collective-permute-start.6 = (bf16[2,256,512]{2,1,0:T(8,128)(2,1)S(1)}, bf16[2,256,512]{2,1,0:T(8,128)(2,1)S(1)}, u32[]{:S(2)}, u32[]{:S(2)}) collective-permute-start(bf16[2,256,512]{2,1,0:T(8,128)(2,1)S(1)} %get-tuple-element.9), channel_id=1, source_target_pairs={{1,4},{2,5},{3,6},{5,8},{6,9},{7,10},{9,12},{10,13},{11,14},{17,20... | collective-permute-start | bytes 1572872 | tf_op jit(solution)/shard_map/ppermute | solution.py:175
  307.4 9.1 %copy-start.6 = (bf16[2,256,512]{2,1,0:T(8,128)(2,1)}, bf16[2,256,512]{2,1,0:T(8,128)(2,1)S(1)}, u32[]{:S(2)}) copy-start(bf16[2,256,512]{2,1,0:T(8,128)(2,1)S(1)} %collective-permute-done.5.refs_6_) | copy-start | bytes 1572868
  316.5 0.8 copy-start.7
  316.5 1.1 copy-start.1
  316.5 1.4 copy-start.2
  316.5 1.6 copy-start.3
  318.1 23.7 %copy-start.8 = (f32[16]{0:T(128)S(1)}, f32[16]{0:T(128)}, u32[]{:S(2)}) copy-start(f32[16]{0:T(128)} %param.15) | copy-start | bytes 196
  334.2 9.5 %collective-permute-start.7 = (bf16[256,512]{1,0:T(8,128)(2,1)S(1)}, bf16[256,512]{1,0:T(8,128)(2,1)S(1)}, u32[]{:S(2)}, u32[]{:S(2)}) collective-permute-start(bf16[256,512]{1,0:T(8,128)(2,1)S(1)} %get-tuple-element.20), channel_id=1, source_target_pairs={{0,1},{1,2},{2,3},{3,0},{4,5},{5,6},{6,7},{7,4},{8,9},{9,10},{10,1... | collective-permute-start | bytes 786440 | tf_op jit(solution)/shard_map/ppermute | solution.py:187
  338.6 11.1 %collective-permute-start.8 = (bf16[256,512]{1,0:T(8,128)(2,1)S(1)}, bf16[256,512]{1,0:T(8,128)(2,1)S(1)}, u32[]{:S(2)}, u32[]{:S(2)}) collective-permute-start(bf16[256,512]{1,0:T(8,128)(2,1)S(1)} %get-tuple-element.19), channel_id=1, source_target_pairs={{0,2},{1,3},{2,0},{3,1},{4,6},{5,7},{6,4},{7,5},{8,10},{9,11},{10,... | collective-permute-start | bytes 786440 | tf_op jit(solution)/shard_map/ppermute | solution.py:187
  338.9 12.7 %collective-permute-start.9 = (bf16[256,512]{1,0:T(8,128)(2,1)S(1)}, bf16[256,512]{1,0:T(8,128)(2,1)S(1)}, u32[]{:S(2)}, u32[]{:S(2)}) collective-permute-start(bf16[256,512]{1,0:T(8,128)(2,1)S(1)} %get-tuple-element.18), channel_id=1, source_target_pairs={{0,3},{1,0},{2,1},{3,2},{4,7},{5,4},{6,5},{7,6},{8,11},{9,8},{10,9... | collective-permute-start | bytes 786440 | tf_op jit(solution)/shard_map/ppermute | solution.py:187

commit v6 on v5

--- a/solution.py
+++ b/solution.py
@@ -250,6 +250,7 @@
     named, packed = lax.optimization_barrier((named, packed))
     own, before = share_heads(packed)
     picked = pick(named.reshape(-1), memory_keys, memory_values, peer_count)
+    picked, own, before = lax.optimization_barrier((picked, own, before))
     arrived = lax.all_to_all(picked, ("grp", "blk"), split_axis=0, concat_axis=0, tiled=True)
     arrived = arrived.reshape(peer_count * capacity, 2, MB, DH)
     band_out = return_rows(band(own, before))

time: 374 us -> 354 us (0.947)
  waiting for transfers between devices: 275 us -> 259 us
  starting transfers between devices: 40.6 us -> 29.3 us
  local copies, waits for them, and re-layouts: 6.47 us -> 10.3 us
    ppermute x4, waiting for transfers between devices: 265 us -> 35.1 us  [share_heads(): before.append(lax.ppermute(packed[shift, 1:], 'blk', pairs))]
    all_to_all x1, waiting for transfers between devices: 0.01 us -> 159 us  [local(): lax.all_to_all(picked, ('grp', 'blk'), split_axis=0, concat_axis=0, tiled...]
    ppermute x3, waiting for transfers between devices: 9.29 us -> 56.8 us  [return_rows(): back.append(lax.ppermute(parts[shift], 'blk', pairs))]
    ppermute x3, waiting for transfers between devices: 0.01 us -> 7.94 us  [share_heads(): lax.ppermute(packed[shift], 'blk', [(i, target(i, shift)) for i in range(...]
    all_to_all x1, starting transfers between devices: 15.9 us -> 8.39 us  [local(): lax.all_to_all(picked, ('grp', 'blk'), split_axis=0, concat_axis=0, tiled...]
  transfers between devices with their start and end apart: 12 -> 12, of which waited for: 7 -> 8; matrix products, arithmetic and copies ran while one was open for 1% -> 2% of each run, Pallas kernels for 5% -> 8%
where the time goes in v6:
time: 354 us; the launch traced here: 349 us
  waiting for transfers between devices  259 us (73%)
  Pallas kernels  46.5 us (13%)
  starting transfers between devices  29.3 us (8%)
  local copies, waits for them, and re-layouts  10.3 us (3%)
    all_to_all x1, waiting for transfers between devices, local(): lax.all_to_all(picked, ('grp', 'blk'), split_axis=0, concat_axis=0, tiled...  159 us
    ppermute x3, waiting for transfers between devices, return_rows(): back.append(lax.ppermute(parts[shift], 'blk', pairs))  56.8 us
    ppermute x4, waiting for transfers between devices, share_heads(): before.append(lax.ppermute(packed[shift, 1:], 'blk', pairs))  35.1 us
    pallas_call x1, Pallas kernels, memory(): pl.pallas_call(memory_kernel, grid_spec=pltpu.PrefetchScalarGridSpec(num_...  18.8 us
    pallas_call x1, Pallas kernels, band(): pl.pallas_call(band_kernel, grid=(width // DH,), out_shape=jax.ShapeDtype...  14.8 us
    pallas_call x1, Pallas kernels, pick(): pl.pallas_call(functools.partial(pick_kernel, peers=peers, each=each), ou...  8.68 us
    all_to_all x1, starting transfers between devices, local(): lax.all_to_all(picked, ('grp', 'blk'), split_axis=0, concat_axis=0, tiled...  8.39 us
    ppermute x3, waiting for transfers between devices, share_heads(): lax.ppermute(packed[shift], 'blk', [(i, target(i, shift)) for i in range(...  7.94 us
  transfers between devices with their start and end apart: 12, of which 8 were waited for; matrix products, arithmetic and copies ran while one was open for 2% of the time, Pallas kernels for 8%

profile of v6, /device:TPU:17, one launch (start us, length us, event | category | flops | bytes accessed | tf_op | source)
XLA Modules:
  0.0 348.8 jit_solution(9216997321540533385)
XLA Ops:
  2.8 6.2 %all-to-all-start = ((s32[32,1,10]{2,1,0:T(1,128)}), s32[32,1,10]{2,1,0:T(1,128)S(1)}, u32[]{:S(2)}, u32[]{:S(2)}) async-start(s32[32,1,10]{2,1,0:T(1,128)} %bitcast.1), calls=%async_computation | async-start | bytes 32768 | tf_op jit(solution)/shard_map/all_to_all | solution.py:249
  9.1 4.2 %pack.1 = bf16[4,3,256,512]{3,2,1,0:T(8,128)(2,1)} custom-call(s32[1]{0:T(128)} %bitcast.member_ref, bf16[256,2048]{1,0:T(8,128)(2,1)} %q_ref.3, bf16[256,2048]{1,0:T(8,128)(2,1)} %k_ref.1, bf16[256,2048]{1,0:T(8,128)(2,1)} %v_ref.1), custom_call_target="tpu_custom_call" | custom-call | tf_op jit(solution)/shard_map/pack/pallas_call | solution.py:150
  13.7 2.8 slice_bitcast_fusion.4
  17.2 1.3 collective-permute-start.4
  18.5 1.7 slice_bitcast_fusion
  20.2 4.1 %collective-permute-start = (bf16[3,256,512]{2,1,0:T(8,128)(2,1)}, bf16[3,256,512]{2,1,0:T(8,128)(2,1)S(1)}, u32[]{:S(2)}, u32[]{:S(2)}) collective-permute-start(bf16[3,256,512]{2,1,0:T(8,128)(2,1)} %get-tuple-element.33), channel_id=1, source_target_pairs={{0,1},{1,2},{2,3},{3,0},{4,5},{5,6},{6,7},{7,4},{8,9},{9,10},{10,1... | collective-permute-start | bytes 2359304 | tf_op jit(solution)/shard_map/ppermute | solution.py:178
  25.3 1.5 collective-permute-start.2
  26.7 1.3 collective-permute-start.5
  28.0 16.5 %collective-permute-done.4.refs_5_ = bf16[2,256,512]{2,1,0:T(8,128)(2,1)S(1)} collective-permute-done((bf16[2,256,512]{2,1,0:T(8,128)(2,1)S(1)}, bf16[2,256,512]{2,1,0:T(8,128)(2,1)S(1)}, u32[]{:S(2)}, u32[]{:S(2)}) %collective-permute-start.4) | collective-permute-done | bytes 524320 | tf_op jit(solution)/shard_map/ppermute | solution.py:175
  45.3 1.3 collective-permute-start.6
  47.3 8.7 %pick.1 = bf16[32,10,2,64,128]{4,3,2,1,0:T(8,128)(2,1)} custom-call(s32[320]{0:T(512)} %reshape.39.req_ref, bf16[8,64,2048]{2,1,0:T(8,128)(2,1)} %key_ref.1, bf16[8,64,2048]{2,1,0:T(8,128)(2,1)} %value_ref.1), custom_call_target="tpu_custom_call" | custom-call | tf_op jit(solution)/shard_map/pick/pallas_call | solution.py:51
  56.0 5.3 %collective-permute-done.5.refs_6_ = bf16[2,256,512]{2,1,0:T(8,128)(2,1)S(1)} collective-permute-done((bf16[2,256,512]{2,1,0:T(8,128)(2,1)}, bf16[2,256,512]{2,1,0:T(8,128)(2,1)S(1)}, u32[]{:S(2)}, u32[]{:S(2)}) %collective-permute-start.5) | collective-permute-done | bytes 524320 | tf_op jit(solution)/shard_map/ppermute | solution.py:175
  61.3 13.3 %collective-permute-done.6.refs_7_ = bf16[2,256,512]{2,1,0:T(8,128)(2,1)} collective-permute-done((bf16[2,256,512]{2,1,0:T(8,128)(2,1)}, bf16[2,256,512]{2,1,0:T(8,128)(2,1)}, u32[]{:S(2)}, u32[]{:S(2)}) %collective-permute-start.6) | collective-permute-done | bytes 524320 | tf_op jit(solution)/shard_map/ppermute | solution.py:175
  74.6 7.9 %collective-permute-done.1.refs_2_ = bf16[3,256,512]{2,1,0:T(8,128)(2,1)S(1)} collective-permute-done((bf16[3,256,512]{2,1,0:T(8,128)(2,1)}, bf16[3,256,512]{2,1,0:T(8,128)(2,1)S(1)}, u32[]{:S(2)}, u32[]{:S(2)}) %collective-permute-start.1) | collective-permute-done | bytes 786464 | tf_op jit(solution)/shard_map/ppermute | solution.py:178
  83.7 8.4 %all-to-all-start.1 = ((bf16[32,10,2,64,128]{4,3,2,1,0:T(8,128)(2,1)}), bf16[32,10,2,64,128]{4,3,2,1,0:T(8,128)(2,1)}, u32[]{:S(2)}, u32[]{:S(2)}) async-start(bf16[32,10,2,64,128]{4,3,2,1,0:T(8,128)(2,1)} %pick.1), calls=%async_computation.1 | async-start | bytes 20971520 | tf_op jit(solution)/shard_map/all_to_all | solution.py:254
  92.1 14.8 %band.1 = bf16[4,256,512]{2,1,0:T(8,128)(2,1)} custom-call(bf16[3,256,512]{2,1,0:T(8,128)(2,1)} %get-tuple-element.18.refs_0_, bf16[3,256,512]{2,1,0:T(8,128)(2,1)} %copy-done.1, bf16[3,256,512]{2,1,0:T(8,128)(2,1)} %copy-done.2, bf16[3,256,512]{2,1,0:T(8,128)(2,1)} %copy-done.3, bf16[2,256,512]{2,1,0:T(8,128)(2,1)} %copy-done.4, ...), custom_call_target="tpu_custom_call" | custom-call | flops 2147483648 | bytes 7340032 | tf_op jit(solution)/shard_map/band/pallas_call | solution.py:118
  107.0 1.3 fusion.1
  108.2 1.2 collective-permute-start.7
  109.5 1.2 collective-permute-start.8
  110.7 1.2 collective-permute-start.9
  113.0 48.0 %collective-permute-done.7 = bf16[256,512]{1,0:T(8,128)(2,1)S(1)} collective-permute-done((bf16[256,512]{1,0:T(8,128)(2,1)S(1)}, bf16[256,512]{1,0:T(8,128)(2,1)S(1)}, u32[]{:S(2)}, u32[]{:S(2)}) %collective-permute-start.7) | collective-permute-done | bytes 262176 | tf_op jit(solution)/shard_map/ppermute | solution.py:187
  161.0 8.8 %collective-permute-done.9 = bf16[256,512]{1,0:T(8,128)(2,1)S(1)} collective-permute-done((bf16[256,512]{1,0:T(8,128)(2,1)S(1)}, bf16[256,512]{1,0:T(8,128)(2,1)S(1)}, u32[]{:S(2)}, u32[]{:S(2)}) %collective-permute-start.9) | collective-permute-done | bytes 262176 | tf_op jit(solution)/shard_map/ppermute | solution.py:187
  170.9 159.1 %all-to-all-done.1 = bf16[32,10,2,64,128]{4,3,2,1,0:T(8,128)(2,1)} async-done(((bf16[32,10,2,64,128]{4,3,2,1,0:T(8,128)(2,1)}), bf16[32,10,2,64,128]{4,3,2,1,0:T(8,128)(2,1)}, u32[]{:S(2)}, u32[]{:S(2)}) %all-to-all-start.1) | async-done | bytes 10485792 | tf_op jit(solution)/shard_map/all_to_all | solution.py:254
  330.0 18.8 %memory.1 = bf16[256,2048]{1,0:T(8,128)(2,1)} custom-call(s32[257]{0:T(512)} %pad_add_fusion.arrival_ref, f32[16]{0:T(128)} %add_divide_fusion.gate_ref, bf16[256,2048]{1,0:T(8,128)(2,1)} %q_ref.3, bf16[4,256,512]{2,1,0:T(8,128)(2,1)} %pad_maximum_fusion.band_ref, ...), custom_call_target="tpu_custom_call" | custom-call | tf_op jit(solution)/shard_map/memory/pallas_call | solution.py:216
  (36 shorter events, 9.8 us)
Async XLA Ops:
  2.8 10.9 %all-to-all-start = ((s32[32,1,10]{2,1,0:T(1,128)}), s32[32,1,10]{2,1,0:T(1,128)S(1)}, u32[]{:S(2)}, u32[]{:S(2)}) async-start(s32[32,1,10]{2,1,0:T(1,128)} %bitcast.1), calls=%async_computation | async-start | bytes 32768 | tf_op jit(solution)/shard_map/all_to_all | solution.py:249
  13.3 5.2 %copy-start = (bf16[4,3,256,512]{3,2,1,0:T(8,128)(2,1)S(1)}, bf16[4,3,256,512]{3,2,1,0:T(8,128)(2,1)}, u32[]{:S(2)}) copy-start(bf16[4,3,256,512]{3,2,1,0:T(8,128)(2,1)} %pack.1) | copy-start | bytes 9437188
  16.5 10.2 %collective-permute-start.3 = (bf16[2,256,512]{2,1,0:T(8,128)(2,1)S(1)}, bf16[2,256,512]{2,1,0:T(8,128)(2,1)S(1)}, u32[]{:S(2)}, u32[]{:S(2)}) collective-permute-start(bf16[2,256,512]{2,1,0:T(8,128)(2,1)S(1)} %get-tuple-element.30), channel_id=1, source_target_pairs={{1,5},{2,6},{3,7},{5,9},{6,10},{7,11},{9,13},{10,14},{11,15},{17,2... | collective-permute-start | bytes 1572872 | tf_op jit(solution)/shard_map/ppermute | solution.py:175
  17.2 27.3 %collective-permute-start.4 = (bf16[2,256,512]{2,1,0:T(8,128)(2,1)S(1)}, bf16[2,256,512]{2,1,0:T(8,128)(2,1)S(1)}, u32[]{:S(2)}, u32[]{:S(2)}) collective-permute-start(bf16[2,256,512]{2,1,0:T(8,128)(2,1)S(1)} %get-tuple-element.29), channel_id=1, source_target_pairs={{1,6},{2,7},{3,4},{5,10},{6,11},{7,8},{9,14},{10,15},{11,12},{17,2... | collective-permute-start | bytes 1572872 | tf_op jit(solution)/shard_map/ppermute | solution.py:175
  20.2 54.4 %collective-permute-start = (bf16[3,256,512]{2,1,0:T(8,128)(2,1)}, bf16[3,256,512]{2,1,0:T(8,128)(2,1)S(1)}, u32[]{:S(2)}, u32[]{:S(2)}) collective-permute-start(bf16[3,256,512]{2,1,0:T(8,128)(2,1)} %get-tuple-element.33), channel_id=1, source_target_pairs={{0,1},{1,2},{2,3},{3,0},{4,5},{5,6},{6,7},{7,4},{8,9},{9,10},{10,1... | collective-permute-start | bytes 2359304 | tf_op jit(solution)/shard_map/ppermute | solution.py:178
  24.4 58.2 %collective-permute-start.1 = (bf16[3,256,512]{2,1,0:T(8,128)(2,1)}, bf16[3,256,512]{2,1,0:T(8,128)(2,1)S(1)}, u32[]{:S(2)}, u32[]{:S(2)}) collective-permute-start(bf16[3,256,512]{2,1,0:T(8,128)(2,1)} %get-tuple-element.32), channel_id=1, source_target_pairs={{0,2},{1,3},{2,0},{3,1},{4,6},{5,7},{6,4},{7,5},{8,10},{9,11},{10,... | collective-permute-start | bytes 2359304 | tf_op jit(solution)/shard_map/ppermute | solution.py:178
  25.3 57.3 %collective-permute-start.2 = (bf16[3,256,512]{2,1,0:T(8,128)(2,1)}, bf16[3,256,512]{2,1,0:T(8,128)(2,1)S(1)}, u32[]{:S(2)}, u32[]{:S(2)}) collective-permute-start(bf16[3,256,512]{2,1,0:T(8,128)(2,1)} %get-tuple-element.31), channel_id=1, source_target_pairs={{0,3},{1,0},{2,1},{3,2},{4,7},{5,4},{6,5},{7,6},{8,11},{9,8},{10,9... | collective-permute-start | bytes 2359304 | tf_op jit(solution)/shard_map/ppermute | solution.py:178
  26.7 17.8 %copy-start.4 = (bf16[2,256,512]{2,1,0:T(8,128)(2,1)}, bf16[2,256,512]{2,1,0:T(8,128)(2,1)S(1)}, u32[]{:S(2)}) copy-start(bf16[2,256,512]{2,1,0:T(8,128)(2,1)S(1)} %collective-permute-done.3.refs_4_) | copy-start | bytes 1572868
  26.7 34.5 %collective-permute-start.5 = (bf16[2,256,512]{2,1,0:T(8,128)(2,1)}, bf16[2,256,512]{2,1,0:T(8,128)(2,1)S(1)}, u32[]{:S(2)}, u32[]{:S(2)}) collective-permute-start(bf16[2,256,512]{2,1,0:T(8,128)(2,1)} %get-tuple-element.28), channel_id=1, source_target_pairs={{1,7},{2,4},{3,5},{5,11},{6,8},{7,9},{9,15},{10,12},{11,13},{17,23... | collective-permute-start | bytes 1572872 | tf_op jit(solution)/shard_map/ppermute | solution.py:175
  44.5 0.8 copy-start.5
  45.3 29.3 %collective-permute-start.6 = (bf16[2,256,512]{2,1,0:T(8,128)(2,1)}, bf16[2,256,512]{2,1,0:T(8,128)(2,1)}, u32[]{:S(2)}, u32[]{:S(2)}) collective-permute-start(bf16[2,256,512]{2,1,0:T(8,128)(2,1)} %get-tuple-element.27), channel_id=1, source_target_pairs={{1,4},{2,5},{3,6},{5,8},{6,9},{7,10},{9,12},{10,13},{11,14},{17,20... | collective-permute-start | bytes 1572872 | tf_op jit(solution)/shard_map/ppermute | solution.py:175
  61.3 21.3 %copy-start.6 = (bf16[2,256,512]{2,1,0:T(8,128)(2,1)}, bf16[2,256,512]{2,1,0:T(8,128)(2,1)S(1)}, u32[]{:S(2)}) copy-start(bf16[2,256,512]{2,1,0:T(8,128)(2,1)S(1)} %collective-permute-done.5.refs_6_) | copy-start | bytes 1572868
  74.6 7.9 %copy-start.1 = (bf16[3,256,512]{2,1,0:T(8,128)(2,1)}, bf16[3,256,512]{2,1,0:T(8,128)(2,1)S(1)}, u32[]{:S(2)}) copy-start(bf16[3,256,512]{2,1,0:T(8,128)(2,1)S(1)} %collective-permute-done.refs_1_) | copy-start | bytes 2359300
  82.5 0.9 copy-start.2
  82.5 1.2 copy-start.3
  83.7 246.3 %all-to-all-start.1 = ((bf16[32,10,2,64,128]{4,3,2,1,0:T(8,128)(2,1)}), bf16[32,10,2,64,128]{4,3,2,1,0:T(8,128)(2,1)}, u32[]{:S(2)}, u32[]{:S(2)}) async-start(bf16[32,10,2,64,128]{4,3,2,1,0:T(8,128)(2,1)} %pick.1), calls=%async_computation.1 | async-start | bytes 20971520 | tf_op jit(solution)/shard_map/all_to_all | solution.py:254
  92.1 20.3 %copy-start.7 = (f32[16]{0:T(128)S(1)}, f32[16]{0:T(128)}, u32[]{:S(2)}) copy-start(f32[16]{0:T(128)} %param.15) | copy-start | bytes 196
  108.2 52.8 %collective-permute-start.7 = (bf16[256,512]{1,0:T(8,128)(2,1)S(1)}, bf16[256,512]{1,0:T(8,128)(2,1)S(1)}, u32[]{:S(2)}, u32[]{:S(2)}) collective-permute-start(bf16[256,512]{1,0:T(8,128)(2,1)S(1)} %get-tuple-element.38), channel_id=1, source_target_pairs={{0,1},{1,2},{2,3},{3,0},{4,5},{5,6},{6,7},{7,4},{8,9},{9,10},{10,1... | collective-permute-start | bytes 786440 | tf_op jit(solution)/shard_map/ppermute | solution.py:187
  109.5 51.5 %collective-permute-start.8 = (bf16[256,512]{1,0:T(8,128)(2,1)S(1)}, bf16[256,512]{1,0:T(8,128)(2,1)S(1)}, u32[]{:S(2)}, u32[]{:S(2)}) collective-permute-start(bf16[256,512]{1,0:T(8,128)(2,1)S(1)} %get-tuple-element.37), channel_id=1, source_target_pairs={{0,2},{1,3},{2,0},{3,1},{4,6},{5,7},{6,4},{7,5},{8,10},{9,11},{10,... | collective-permute-start | bytes 786440 | tf_op jit(solution)/shard_map/ppermute | solution.py:187
  110.7 59.1 %collective-permute-start.9 = (bf16[256,512]{1,0:T(8,128)(2,1)S(1)}, bf16[256,512]{1,0:T(8,128)(2,1)S(1)}, u32[]{:S(2)}, u32[]{:S(2)}) collective-permute-start(bf16[256,512]{1,0:T(8,128)(2,1)S(1)} %get-tuple-element.36), channel_id=1, source_target_pairs={{0,3},{1,0},{2,1},{3,2},{4,7},{5,4},{6,5},{7,6},{8,11},{9,8},{10,9... | collective-permute-start | bytes 786440 | tf_op jit(solution)/shard_map/ppermute | solution.py:187
